TPU v7x, 128 devices: a whole 4x4x4 slice. The times are simulated.
128 devices in a mesh: tm: 4 (over z), col: 32 (over x, y, core).
Axes of the slice: x: 4, y: 4, z: 4, core: 2. Of those that a mesh axis runs over, the one named last changes fastest.
Arguments:
- forcing_state: float32 [4, 5, 64, 4, 8192], P('tm', None, None, None, 'col'), may hold values from -6 to 6
- model_error: float32 [4, 5, 64, 4, 8192], P('tm', None, None, None, 'col'), may hold values from 0.3 to 3
- courant: float32 [4, 4, 64, 4, 8192], P('tm', None, None, None, 'col'), may hold values from 0.2 to 0.9
- vertical_mix: float32 [5, 64, 64], replicated, may hold values from -0.75 to 0.75
- radiance_jacobian: float32 [320, 128], replicated, may hold values from -0.3125 to 0.3125
- innovation: float32 [4, 16384, 128], P('tm', 'col'), may hold values from -6 to 6
- report_error: float32 [4, 16384, 128], P('tm', 'col'), may hold values from 0.3 to 3
- report_column: int32 [4, 16384], P('tm', 'col'), may hold values from 0 to 32767, as said below
- report_slot: int32 [4, 16384], P('tm', 'col'), may hold values from 0 to 3
- report_count: int32 [4, 32, 4], P('tm', 'col'), may hold values from 32 to 128
Outputs:
- model_dual: float32 [4, 5, 64, 4, 8192], P('tm', None, None, None, 'col')
- report_dual: float32 [4, 16384, 128], P('tm', 'col')
- increment: float32 [4, 5, 64, 4, 8192], P('tm', None, None, None, 'col')
- model_residual: float32 [4, 5, 64, 4, 8192], P('tm', None, None, None, 'col')
- report_residual: float32 [4, 16384, 128], P('tm', 'col')
- increment_residual: float32 [4, 5, 64, 4, 8192], P('tm', None, None, None, 'col')
Inputs may be any that keep to these rules, and one draw needn't show every extreme that they name: `report_column`: on each device and in each section, the rows name grid columns in at most 32 of one block of 256 columns (the block that one index of col holds); in every section one block receives exactly 32 rows from every device.
All inputs are finite; a program needn't handle non-finite values.
Results may differ from a plain program's by a relative error of at most 0.00013.
Values sent between devices are 32-bit elements; how exact they have to be, the bound alone decides.
A program may use at most 128 MiB of HBM per device.

v0:
```python
import jax
import jax.numpy as jnp
from jax import lax
from jax.sharding import PartitionSpec as P

ITERATIONS = 2


def shifted(block, axis, distance):
    devices = range(lax.axis_size(axis))
    route = [((i - distance) % len(devices), i) for i in devices]
    return lax.ppermute(block, axis, route)


def from_behind(value, axis, steps):
    count = lax.axis_size(axis)
    initial, last = (max(0, -steps), min(count, count - steps))
    return lax.ppermute(value, axis, [(source, source + steps) for source in range(initial, last)])


def apply_mix(mixer, values):
    return jnp.einsum("fkl,flyx->fkyx", mixer, values, precision=lax.Precision.HIGHEST)


def advect_step(values, courant_now, mixer):
    block_width = values.shape[3]
    left_edge = shifted(values[..., -1:], "col", 1)
    first_column = jnp.arange(block_width, dtype=jnp.int32) == 0
    before = jnp.where(first_column, left_edge, jnp.roll(values, 1, axis=3))
    return apply_mix(mixer, values - courant_now * (values - before))


def adjoint_step(values, courant_now, mixer):
    block_width = values.shape[3]
    mixed_back = jnp.einsum("flk,flyx->fkyx", mixer, values, precision=lax.Precision.HIGHEST)
    carried = courant_now * mixed_back
    right_edge = shifted(carried[..., :1], "col", -1)
    last_column = jnp.arange(block_width, dtype=jnp.int32) == block_width - 1
    after = jnp.where(last_column, right_edge, jnp.roll(carried, -1, axis=3))
    return mixed_back - carried + after


def forward_steps(values, wind_field, mixer):
    slot_states = []
    for moment in range(wind_field.shape[0]):
        slot_states.append(values)
        values = advect_step(values, wind_field[moment], mixer)
    return (jnp.stack(slot_states), values)


def body(
    forcing_state,
    model_error,
    courant,
    vertical_mix,
    radiance_jacobian,
    innovation,
    report_error,
    report_column,
    report_slot,
    report_count,
):
    forcing = forcing_state[0]
    variance = model_error[0]
    wind_field = courant[0]
    fields, levels, lat_rows, block_width = forcing.shape
    step_count = wind_field.shape[0]
    profile = fields * levels
    cell_count = lat_rows * block_width
    mixer = 0.6 * jnp.eye(levels, dtype=jnp.float32)[None] + 0.4 * vertical_mix
    owners = lax.axis_size("col")
    report_rows = report_column.shape[1]
    capacity = 2 * report_rows // owners
    counts = report_count[0, 0]
    inst_rows = report_rows // counts.shape[0]
    inside = jnp.arange(inst_rows, dtype=jnp.int32)[None, :] < counts[:, None]
    weights = inside.reshape(report_rows).astype(jnp.float32)
    column = report_column[0]
    grid_width = block_width * owners
    east_index = column % grid_width
    north_index = column // grid_width
    owner_block = east_index // block_width
    cell_index = north_index * block_width + east_index % block_width
    onehot = (owner_block[:, None] == jnp.arange(owners, dtype=jnp.int32)[None, :]).astype(
        jnp.int32
    )
    ranking = jnp.sum(jnp.cumsum(onehot, axis=0) * onehot, axis=1) - 1
    landing = owner_block * capacity + ranking

    def to_owner_slots(payload):
        buffer = (
            jnp.zeros((owners * capacity, payload.shape[1]), payload.dtype).at[landing].set(payload)
        )
        return buffer.reshape(owners, capacity, payload.shape[1])

    payload = jnp.stack(
        [cell_index, report_slot[0], inside.reshape(report_rows).astype(jnp.int32)], axis=1
    )
    received = lax.all_to_all(
        to_owner_slots(payload), "col", split_axis=0, concat_axis=0, tiled=True
    ).reshape(owners * capacity, 3)
    slot_ids = received[:, 1]
    cell_ids = received[:, 0]
    filled = received[:, 2].astype(jnp.float32)[:, None]
    report_var = report_error[0]
    model_res = forcing
    report_res = weights[:, None] * innovation[0]
    incr_res = jnp.zeros_like(forcing)
    model_sol = jnp.zeros_like(forcing)
    report_sol = jnp.zeros_like(report_res)
    incr_sol = jnp.zeros_like(forcing)
    for iteration in range(ITERATIONS):
        history, closing = forward_steps(incr_res, wind_field, mixer)
        arriving = from_behind(closing, "tm", 1)
        upper_block = variance * model_res + incr_res - arriving
        flat_history = history.reshape(step_count, profile, cell_count)
        picked = flat_history[slot_ids, :, cell_ids] * filled
        returned = lax.all_to_all(
            picked.reshape(owners, capacity, profile),
            "col",
            split_axis=0,
            concat_axis=0,
            tiled=True,
        )
        observed = jnp.dot(
            returned.reshape(owners * capacity, profile)[landing],
            radiance_jacobian,
            precision=lax.Precision.HIGHEST,
        )
        middle = weights[:, None] * (report_var * report_res + observed)
        weighted = weights[:, None] * report_res
        spread_rows = jnp.dot(weighted, radiance_jacobian.T, precision=lax.Precision.HIGHEST)
        spread = lax.all_to_all(
            to_owner_slots(spread_rows), "col", split_axis=0, concat_axis=0, tiled=True
        ).reshape(owners * capacity, profile)
        inject = (
            jnp.zeros((step_count, profile, cell_count), jnp.float32)
            .at[slot_ids, :, cell_ids]
            .add(spread * filled)
        )
        inject = inject.reshape(step_count, fields, levels, lat_rows, block_width)
        later_dual = from_behind(model_res, "tm", -1)
        adjoint = -later_dual
        for moment in reversed(range(step_count)):
            adjoint = adjoint_step(adjoint, wind_field[moment], mixer) + inject[moment]
        upper_block, middle, lower = (upper_block, middle, model_res + adjoint)
        local_projection = (
            jnp.sum(model_res * upper_block)
            + jnp.sum(report_res * middle)
            + jnp.sum(incr_res * lower)
        )
        local_energy = (
            jnp.sum(upper_block * upper_block) + jnp.sum(middle * middle) + jnp.sum(lower * lower)
        )
        projection, energy = lax.psum((local_projection, local_energy), ("tm", "col"))
        step_size = projection / energy
        model_sol = model_sol + step_size * model_res
        report_sol = report_sol + step_size * report_res
        incr_sol = incr_sol + step_size * incr_res
        model_res = model_res - step_size * upper_block
        report_res = report_res - step_size * middle
        incr_res = incr_res - step_size * lower
    return (
        model_sol[None],
        report_sol[None],
        incr_sol[None],
        model_res[None],
        report_res[None],
        incr_res[None],
    )


def solution(mesh):
    in_specs = (
        P("tm", None, None, None, "col"),
        P("tm", None, None, None, "col"),
        P("tm", None, None, None, "col"),
        P(),
        P(),
        P("tm", "col", None),
        P("tm", "col", None),
        P("tm", "col"),
        P("tm", "col"),
        P("tm", "col", None),
    )
    out_specs = (
        P("tm", None, None, None, "col"),
        P("tm", "col", None),
        P("tm", None, None, None, "col"),
        P("tm", None, None, None, "col"),
        P("tm", "col", None),
        P("tm", None, None, None, "col"),
    )
    return jax.shard_map(body, mesh=mesh, in_specs=in_specs, out_specs=out_specs, check_vma=False)
```

profile of v0, /device:TPU:1, one launch (start us, length us, event | category | flops | bytes accessed | tf_op | source)
XLA Modules:
  0.0 674.5 jit_solution(16760754805494352969)
XLA Ops:
  8.8 8.6 %all-to-all-start = ((s32[32,32,3]{1,2,0:T(4,128)}), s32[32,32,3]{1,2,0:T(4,128)S(1)}, u32[]{:S(2)}, u32[]{:S(2)}) async-start(s32[32,32,3]{1,2,0:T(4,128)} %copy.250), calls=%async_computation | async-start | bytes 131072 | tf_op jit(solution)/shard_map/all_to_all | solution.py:99
  27.5 4.5 scatter_custom_fusion.1
  39.6 2.9 fusion.7
  49.6 8.5 %all-to-all-start.2 = ((f32[32,32,320]{2,1,0:T(8,128)}), f32[32,32,320]{2,1,0:T(8,128)}, u32[]{:S(2)}, u32[]{:S(2)}) async-start(f32[32,32,320]{2,1,0:T(8,128)} %bitcast.239), calls=%async_computation.2 | async-start | bytes 3145728 | tf_op jit(solution)/shard_map/all_to_all | solution.py:133
  58.6 2.9 fusion.14
  65.8 2.8 stack.34
  68.6 3.0 copy.247
  71.5 5.5 pad_maximum_fusion
  77.0 23.6 %gather_fusion = f32[1024,320]{1,0:T(8,128)} fusion(f32[4,320,1024]{1,2,0:T(8,128)} %pad_maximum_fusion, s32[1024]{0:T(1024)S(1)} %bitcast.224), kind=kCustom, calls=%fused_computation | custom fusion | bytes 2629632 | tf_op jit(solution)/shard_map/gather | solution.py:117
  100.6 2.8 broadcast_multiply_fusion.1
  103.4 2.8 fusion.21
  106.2 17.2 %collective-permute-start.4 = (f32[5,64,4,256]{3,1,2,0:T(8,128)}, f32[5,64,4,256]{3,1,2,0:T(8,128)}, u32[]{:S(2)}, u32[]{:S(2)}) collective-permute-start(f32[5,64,4,256]{3,1,2,0:T(8,128)} %fusion.21), channel_id=1, source_target_pairs={{0,32},{32,64},{64,96},{1,33},{33,65},{65,97},{2,34},{34,66},{66,9... | collective-permute-start | bytes 3932168 | tf_op jit(solution)/shard_map/ppermute | solution.py:18
  123.4 13.9 %all-to-all-start.1 = ((f32[32,32,320]{2,1,0:T(8,128)}), f32[32,32,320]{2,1,0:T(8,128)S(1)}, u32[]{:S(2)}, u32[]{:S(2)}) async-start(f32[32,32,320]{2,1,0:T(8,128)} %broadcast_multiply_fusion.1), calls=%async_computation.1 | async-start | bytes 3145728 | tf_op jit(solution)/shard_map/all_to_all | solution.py:118
  137.3 2.8 bitcast_multiply_fusion.1
  140.1 10.2 %scatter_custom_fusion.3 = f32[4096,320]{1,0:T(8,128)} fusion(s32[1024]{0:T(1024)S(1)} %broadcast_select_fusion, f32[1024,320]{1,0:T(8,128)} %bitcast_multiply_fusion.1, f32[]{:T(128)} %constant.69.clone.1), kind=kCustom, calls=%fused_computation.13 | custom fusion | flops 327680 | bytes 5243392
  150.3 7.8 %copy.315 = f32[4,1024,320]{1,0,2:T(4,128)} copy(f32[4,1024,320]{2,1,0:T(8,128)} %bitcast.236) | data formatting | bytes 10485760
  158.1 3.6 broadcast_multiply_fusion.3
  163.6 24.4 %slice_reduce_fusion.4 = (f32[320,1024]{1,0:T(8,128)}, f32[320,1024]{1,0:T(8,128)}, f32[320,1024]{1,0:T(8,128)}, f32[320,1024]{1,0:T(8,128)}) fusion(f32[4,320,1024]{2,0,1:T(4,128)} %bitcast.237), kind=kLoop, calls=%fused_computation.21 | loop fusion | bytes 10485760 | tf_op jit(solution)/shard_map/slice | solution.py:145
  188.0 2.8 squeeze.54
  192.7 4.4 broadcast_multiply_fusion.5
  198.4 5.4 collective-permute-start.7
  203.8 2.8 squeeze.55
  208.6 4.4 broadcast_multiply_fusion.7
  217.1 2.8 squeeze.57
  226.9 4.4 broadcast_multiply_fusion.9
  238.2 5.7 multiply_reduce_fusion.4
  247.7 62.3 %all-reduce.1 = (f32[]{:T(128)}, f32[]{:T(128)}) all-reduce(f32[]{:T(128)S(6)} %add.251, f32[]{:T(128)S(6)} %add.253), channel_id=1, replica_groups=mesh['tm'=4,'col'=32] {'tm','col'}, use_global_device_ids=true, to_apply=%region_9.10 | all-reduce | flops 2 | bytes 16 | tf_op jit(solution)/shard_map/psum | solution.py:155
  313.4 3.4 scatter_custom_fusion.2
  316.8 5.4 all-to-all-start.4
  325.8 19.2 %all-to-all-done.4 = f32[32,32,320]{2,1,0:T(8,128)} async-done(((f32[32,32,320]{2,1,0:T(8,128)}), f32[32,32,320]{2,1,0:T(8,128)}, u32[]{:S(2)}, u32[]{:S(2)}) %all-to-all-start.4) | async-done | bytes 1310752 | tf_op jit(solution)/shard_map/all_to_all | solution.py:133
  347.7 10.2 %scatter_custom_fusion.4 = f32[4096,320]{1,0:T(8,128)} fusion(s32[1024]{0:T(1024)S(1)} %broadcast_select_fusion, f32[1024,320]{1,0:T(8,128)} %bitcast_multiply_fusion, f32[]{:T(128)} %constant.69.clone.1), kind=kCustom, calls=%fused_computation.11 | custom fusion | flops 327680 | bytes 5243392
  357.9 7.8 %copy.324 = f32[4,1024,320]{1,0,2:T(4,128)} copy(f32[4,1024,320]{2,1,0:T(8,128)} %bitcast.235) | data formatting | bytes 10485760
  370.3 24.4 %slice_reduce_fusion = (f32[320,1024]{1,0:T(8,128)}, f32[320,1024]{1,0:T(8,128)}, f32[320,1024]{1,0:T(8,128)}, f32[320,1024]{1,0:T(8,128)}) fusion(f32[4,320,1024]{2,0,1:T(4,128)} %bitcast.238), kind=kLoop, calls=%fused_computation.17 | loop fusion | bytes 10485760 | tf_op jit(solution)/shard_map/slice | solution.py:145
  394.8 2.8 squeeze.58
  399.4 4.4 broadcast_multiply_fusion.4
  406.8 2.8 squeeze.59
  411.4 4.4 broadcast_multiply_fusion.6
  418.2 2.8 squeeze.60
  423.0 3.1 broadcast_multiply_fusion.8
  429.3 2.9 squeeze.61
  433.7 4.6 multiply_reduce_fusion
  441.1 2.8 fusion.49
  447.4 5.5 collective-permute-done.11
  453.0 3.7 fusion.56
  461.0 2.8 stack.37
  463.9 3.0 copy.274
  466.8 3.2 copy.271
  470.0 2.8 stack.38
  472.8 3.0 copy.275
  477.8 2.8 stack.39
  480.6 3.0 copy.276
  483.6 2.8 fusion.63
  489.9 2.8 stack.40
  492.7 3.1 copy.277
  495.8 4.4 pad_maximum_fusion.1
  500.2 18.3 %gather_fusion.2 = f32[1024,320]{1,0:T(8,128)S(1)} fusion(f32[4,320,1024]{1,2,0:T(8,128)} %pad_maximum_fusion.1, s32[1024]{0:T(1024)S(1)} %bitcast.225), kind=kCustom, calls=%fused_computation.2 | custom fusion | bytes 2629632 | tf_op jit(solution)/shard_map/gather | solution.py:117
  520.0 31.6 %all-to-all-start.3 = ((f32[32,32,320]{2,1,0:T(8,128)}), f32[32,32,320]{2,1,0:T(8,128)S(1)}, u32[]{:S(2)}, u32[]{:S(2)}) async-start(f32[32,32,320]{2,1,0:T(8,128)} %broadcast_multiply_fusion), calls=%async_computation.3 | async-start | bytes 3145728 | tf_op jit(solution)/shard_map/all_to_all | solution.py:118
  551.6 4.8 fusion.70
  558.7 15.6 %all-to-all-done.3 = f32[32,32,320]{2,1,0:T(8,128)S(1)} async-done(((f32[32,32,320]{2,1,0:T(8,128)}), f32[32,32,320]{2,1,0:T(8,128)S(1)}, u32[]{:S(2)}, u32[]{:S(2)}) %all-to-all-start.3) | async-done | bytes 1310752 | tf_op jit(solution)/shard_map/all_to_all | solution.py:118
  576.6 2.8 multiply_reduce_fusion.8
  579.4 6.9 %collective-permute-done.14 = f32[5,64,4,256]{3,1,2,0:T(8,128)} collective-permute-done((f32[5,64,4,256]{3,1,2,0:T(8,128)}, f32[5,64,4,256]{3,1,2,0:T(8,128)}, u32[]{:S(2)}, u32[]{:S(2)}) %collective-permute-start.14) | collective-permute-done | bytes 1310752 | tf_op jit(solution)/shard_map/ppermute | solution.py:18
  586.2 3.9 multiply_reduce_fusion.1
  594.0 67.4 %all-reduce = (f32[]{:T(128)}, f32[]{:T(128)}) all-reduce(f32[]{:T(128)S(6)} %add.266, f32[]{:T(128)S(6)} %add.268), channel_id=1, replica_groups=mesh['tm'=4,'col'=32] {'tm','col'}, use_global_device_ids=true, to_apply=%region_19.20 | all-reduce | flops 2 | bytes 16 | tf_op jit(solution)/shard_map/psum | solution.py:155
  662.7 3.0 subtract_bitcast_fusion
  (257 shorter events, 121.7 us)
Async XLA Ops:
  0.6 21.5 %copy-start = (f32[320,128]{1,0:T(8,128)S(1)}, f32[320,128]{1,0:T(8,128)}, u32[]{:S(2)}) copy-start(f32[320,128]{1,0:T(8,128)} %param.14) | copy-start | bytes 491524
  0.6 16.7 %copy-start.3 = (f32[1,5,64,4,256]{4,3,2,1,0:T(4,128)S(1)}, f32[1,5,64,4,256]{4,3,2,1,0:T(4,128)}, u32[]{:S(2)}) copy-start(f32[1,5,64,4,256]{4,3,2,1,0:T(4,128)} %param.10) | copy-start | bytes 3932164
  6.1 21.4 %copy-start.53 = (s32[512,1]{0,1:T(1,128)}, s32[512,1]{0,1:T(1,128)S(1)}, u32[]{:S(2)}) copy-start(s32[512,1]{0,1:T(1,128)S(1)} %compare_select_fusion.2) | copy-start | bytes 6148
  8.8 40.8 %all-to-all-start = ((s32[32,32,3]{1,2,0:T(4,128)}), s32[32,32,3]{1,2,0:T(4,128)S(1)}, u32[]{:S(2)}, u32[]{:S(2)}) async-start(s32[32,32,3]{1,2,0:T(4,128)} %copy.250), calls=%async_computation | async-start | bytes 131072 | tf_op jit(solution)/shard_map/all_to_all | solution.py:99
  17.4 4.5 copy-start.50
  18.7 3.3 copy-start.52
  18.7 3.4 copy-start.44
  18.7 139.3 %collective-permute-start.5 = (f32[5,64,4,256]{3,1,2,0:T(8,128)}, f32[5,64,4,256]{3,1,2,0:T(8,128)}, u32[]{:S(2)}, u32[]{:S(2)}) collective-permute-start(f32[5,64,4,256]{3,1,2,0:T(8,128)} %bitcast.216), channel_id=1, source_target_pairs={{32,0},{64,32},{96,64},{33,1},{65,33},{97,65},{34,2},{66,34},{98,6... | collective-permute-start | bytes 3932168 | tf_op jit(solution)/shard_map/ppermute | solution.py:18
  20.1 3.7 collective-permute-start
  25.5 7.2 %copy-start.28 = (f32[5,64,4,1]{3,1,2,0:T(8,128)}, f32[5,64,4,1]{3,1,2,0:T(8,128)S(1)}, u32[]{:S(2)}) copy-start(f32[5,64,4,1]{3,1,2,0:T(8,128)S(1)} %slice.245) | copy-start | bytes 15364
  26.4 13.2 %collective-permute-start.1 = (f32[5,64,4,1]{1,2,3,0:T(4,128)}, f32[5,64,4,1]{1,2,3,0:T(4,128)}, u32[]{:S(2)}, u32[]{:S(2)}) collective-permute-start(f32[5,64,4,1]{1,2,3,0:T(4,128)} %copy.237), channel_id=1, source_target_pairs={{31,0},{0,1},{1,2},{2,3},{3,4},{4,5},{5,6},{6,7},{7,8},{8,9},{9,10... | collective-permute-start | bytes 15368 | tf_op jit(solution)/shard_map/ppermute | solution.py:12
  42.7 1.9 copy-start.26
  45.5 13.1 %collective-permute-start.2 = (f32[5,64,4,1]{1,2,3,0:T(4,128)}, f32[5,64,4,1]{1,2,3,0:T(4,128)}, u32[]{:S(2)}, u32[]{:S(2)}) collective-permute-start(f32[5,64,4,1]{1,2,3,0:T(4,128)} %copy.239), channel_id=1, source_target_pairs={{31,0},{0,1},{1,2},{2,3},{3,4},{4,5},{5,6},{6,7},{7,8},{8,9},{9,10... | collective-permute-start | bytes 15368 | tf_op jit(solution)/shard_map/ppermute | solution.py:12
  49.6 8.7 %copy-start.57 = (s32[2]{0:T(128)S(1)}, s32[2]{0:T(128)}, u32[]{:S(2)}) copy-start(s32[2]{0:T(128)} %constant.94) | copy-start | bytes 28
  49.6 8.8 %copy-start.56 = (s32[2]{0:T(128)S(1)}, s32[2]{0:T(128)}, u32[]{:S(2)}) copy-start(s32[2]{0:T(128)} %constant.91) | copy-start | bytes 28
  49.6 73.8 %all-to-all-start.2 = ((f32[32,32,320]{2,1,0:T(8,128)}), f32[32,32,320]{2,1,0:T(8,128)}, u32[]{:S(2)}, u32[]{:S(2)}) async-start(f32[32,32,320]{2,1,0:T(8,128)} %bitcast.239), calls=%async_computation.2 | async-start | bytes 3145728 | tf_op jit(solution)/shard_map/all_to_all | solution.py:133
  63.9 39.5 %collective-permute-start.3 = (f32[5,64,4,1]{1,2,3,0:T(4,128)S(1)}, f32[5,64,4,1]{1,2,3,0:T(4,128)S(1)}, u32[]{:S(2)}, u32[]{:S(2)}) collective-permute-start(f32[5,64,4,1]{1,2,3,0:T(4,128)S(1)} %copy.241), channel_id=1, source_target_pairs={{31,0},{0,1},{1,2},{2,3},{3,4},{4,5},{5,6},{6,7},{7,8},{8,9},{9,10... | collective-permute-start | bytes 15368 | tf_op jit(solution)/shard_map/ppermute | solution.py:12
  68.6 3.0 copy-start.55
  106.2 130.7 %collective-permute-start.4 = (f32[5,64,4,256]{3,1,2,0:T(8,128)}, f32[5,64,4,256]{3,1,2,0:T(8,128)}, u32[]{:S(2)}, u32[]{:S(2)}) collective-permute-start(f32[5,64,4,256]{3,1,2,0:T(8,128)} %fusion.21), channel_id=1, source_target_pairs={{0,32},{32,64},{64,96},{1,33},{33,65},{65,97},{2,34},{34,66},{66,9... | collective-permute-start | bytes 3932168 | tf_op jit(solution)/shard_map/ppermute | solution.py:18
  123.4 99.3 %all-to-all-start.1 = ((f32[32,32,320]{2,1,0:T(8,128)}), f32[32,32,320]{2,1,0:T(8,128)S(1)}, u32[]{:S(2)}, u32[]{:S(2)}) async-start(f32[32,32,320]{2,1,0:T(8,128)} %broadcast_multiply_fusion.1), calls=%async_computation.1 | async-start | bytes 3145728 | tf_op jit(solution)/shard_map/all_to_all | solution.py:118
  163.1 29.6 %collective-permute-start.6 = (f32[5,64,4,1]{1,2,3,0:T(4,128)S(1)}, f32[5,64,4,1]{1,2,3,0:T(4,128)S(1)}, u32[]{:S(2)}, u32[]{:S(2)}) collective-permute-start(f32[5,64,4,1]{1,2,3,0:T(4,128)S(1)} %copy.253), channel_id=1, source_target_pairs={{1,0},{2,1},{3,2},{4,3},{5,4},{6,5},{7,6},{8,7},{9,8},{10,9},{11,1... | collective-permute-start | bytes 15368 | tf_op jit(solution)/shard_map/ppermute | solution.py:12
  198.2 5.7 copy-start.34
  198.4 10.1 %collective-permute-start.7 = (f32[5,64,4,1]{1,2,3,0:T(4,128)S(1)}, f32[5,64,4,1]{1,2,3,0:T(4,128)S(1)}, u32[]{:S(2)}, u32[]{:S(2)}) collective-permute-start(f32[5,64,4,1]{1,2,3,0:T(4,128)S(1)} %copy.258), channel_id=1, source_target_pairs={{1,0},{2,1},{3,2},{4,3},{5,4},{6,5},{7,6},{8,7},{9,8},{10,9},{11,1... | collective-permute-start | bytes 15368 | tf_op jit(solution)/shard_map/ppermute | solution.py:12
  206.6 1.9 copy-start.11
  206.6 1.9 copy-start.35
  206.6 2.0 copy-start.40
  213.0 4.1 copy-start.54
  216.3 10.5 %collective-permute-start.8 = (f32[5,64,4,1]{1,2,3,0:T(4,128)S(1)}, f32[5,64,4,1]{1,2,3,0:T(4,128)S(1)}, u32[]{:S(2)}, u32[]{:S(2)}) collective-permute-start(f32[5,64,4,1]{1,2,3,0:T(4,128)S(1)} %copy.261), channel_id=1, source_target_pairs={{1,0},{2,1},{3,2},{4,3},{5,4},{6,5},{7,6},{8,7},{9,8},{10,9},{11,1... | collective-permute-start | bytes 15368 | tf_op jit(solution)/shard_map/ppermute | solution.py:12
  224.9 1.9 copy-start.30
  224.9 1.9 copy-start.38
  231.2 3.1 copy-start.45
  231.2 3.1 copy-start.49
  231.2 3.1 copy-start.51
  232.3 2.0 copy-start.31
  232.6 3.9 copy-start.19
  232.6 4.3 collective-permute-start.9
  312.5 4.3 copy-start.47
  316.8 28.1 %all-to-all-start.4 = ((f32[32,32,320]{2,1,0:T(8,128)}), f32[32,32,320]{2,1,0:T(8,128)}, u32[]{:S(2)}, u32[]{:S(2)}) async-start(f32[32,32,320]{2,1,0:T(8,128)} %bitcast.240), calls=%async_computation.4 | async-start | bytes 3145728 | tf_op jit(solution)/shard_map/all_to_all | solution.py:133
  324.5 108.2 %copy-start.6 = (f32[5,64,4,256]{3,1,2,0:T(8,128)}, f32[5,64,4,256]{3,1,2,0:T(8,128)S(1)}, u32[]{:S(2)}) copy-start(f32[5,64,4,256]{3,1,2,0:T(8,128)S(1)} %multiply_subtract_fusion.1) | copy-start | bytes 3932164
  324.5 41.2 %collective-permute-start.15 = (f32[5,64,4,256]{3,1,2,0:T(8,128)S(1)}, f32[5,64,4,256]{3,1,2,0:T(8,128)S(1)}, u32[]{:S(2)}, u32[]{:S(2)}) collective-permute-start(f32[5,64,4,256]{3,1,2,0:T(8,128)S(1)} %multiply_subtract_fusion.1), channel_id=1, source_target_pairs={{32,0},{64,32},{96,64},{33,1},{65,33},{97,65},{34,2},{66,34},{98,6... | collective-permute-start | bytes 3932168 | tf_op jit(solution)/shard_map/ppermute | solution.py:18
  369.4 30.0 %collective-permute-start.16 = (f32[5,64,4,1]{1,2,3,0:T(4,128)S(1)}, f32[5,64,4,1]{1,2,3,0:T(4,128)S(1)}, u32[]{:S(2)}, u32[]{:S(2)}) collective-permute-start(f32[5,64,4,1]{1,2,3,0:T(4,128)S(1)} %copy.279), channel_id=1, source_target_pairs={{1,0},{2,1},{3,2},{4,3},{5,4},{6,5},{7,6},{8,7},{9,8},{10,9},{11,1... | collective-permute-start | bytes 15368 | tf_op jit(solution)/shard_map/ppermute | solution.py:12
  405.2 6.2 collective-permute-start.17
  417.2 5.6 collective-permute-start.18
  420.9 1.9 copy-start.42
  420.9 2.1 copy-start.43
  427.2 2.1 copy-start.32
  427.5 5.1 collective-permute-start.19
  429.3 2.9 copy-start.21
  438.5 2.5 copy-start.29
  438.8 2.3 collective-permute-start.10
  443.9 9.1 %copy-start.2 = (f32[5,64,4,256]{3,1,2,0:T(8,128)}, f32[5,64,4,256]{3,1,2,0:T(8,128)S(1)}, u32[]{:S(2)}) copy-start(f32[5,64,4,256]{3,1,2,0:T(8,128)S(1)} %fusion.49) | copy-start | bytes 3932164
  443.9 9.1 %copy-start.13 = (f32[64,4,256]{2,0,1:T(8,128)S(1)}, f32[64,4,256]{2,0,1:T(8,128)}, u32[]{:S(2)}) copy-start(f32[64,4,256]{2,0,1:T(8,128)} %copy.236) | copy-start | bytes 786436
  446.3 6.6 collective-permute-start.11
  459.1 24.5 %collective-permute-start.12 = (f32[5,64,4,1]{1,2,3,0:T(4,128)S(1)}, f32[5,64,4,1]{1,2,3,0:T(4,128)S(1)}, u32[]{:S(2)}, u32[]{:S(2)}) collective-permute-start(f32[5,64,4,1]{1,2,3,0:T(4,128)S(1)} %copy.268), channel_id=1, source_target_pairs={{31,0},{0,1},{1,2},{2,3},{3,4},{4,5},{5,6},{6,7},{7,8},{8,9},{9,10... | collective-permute-start | bytes 15368 | tf_op jit(solution)/shard_map/ppermute | solution.py:12
  480.6 3.0 copy-start.10
  487.5 1.9 copy-start.27
  489.6 62.0 %collective-permute-start.13 = (f32[5,64,4,1]{1,2,3,0:T(4,128)S(1)}, f32[5,64,4,1]{1,2,3,0:T(4,128)S(1)}, u32[]{:S(2)}, u32[]{:S(2)}) collective-permute-start(f32[5,64,4,1]{1,2,3,0:T(4,128)S(1)} %copy.269), channel_id=1, source_target_pairs={{31,0},{0,1},{1,2},{2,3},{3,4},{4,5},{5,6},{6,7},{7,8},{8,9},{9,10... | collective-permute-start | bytes 15368 | tf_op jit(solution)/shard_map/ppermute | solution.py:12
  492.7 3.1 copy-start.25
  520.0 54.3 %all-to-all-start.3 = ((f32[32,32,320]{2,1,0:T(8,128)}), f32[32,32,320]{2,1,0:T(8,128)S(1)}, u32[]{:S(2)}, u32[]{:S(2)}) async-start(f32[32,32,320]{2,1,0:T(8,128)} %broadcast_multiply_fusion), calls=%async_computation.3 | async-start | bytes 3145728 | tf_op jit(solution)/shard_map/all_to_all | solution.py:118
  556.4 29.8 %collective-permute-start.14 = (f32[5,64,4,256]{3,1,2,0:T(8,128)}, f32[5,64,4,256]{3,1,2,0:T(8,128)}, u32[]{:S(2)}, u32[]{:S(2)}) collective-permute-start(f32[5,64,4,256]{3,1,2,0:T(8,128)} %fusion.70), channel_id=1, source_target_pairs={{0,32},{32,64},{64,96},{1,33},{33,65},{65,97},{2,34},{34,66},{66,9... | collective-permute-start | bytes 3932168 | tf_op jit(solution)/shard_map/ppermute | solution.py:18
  574.3 2.3 copy-start.48
  576.6 9.7 %copy-start.7 = (f32[5,64,4,256]{3,1,2,0:T(8,128)S(1)}, f32[5,64,4,256]{3,1,2,0:T(8,128)}, u32[]{:S(2)}) copy-start(f32[5,64,4,256]{3,1,2,0:T(8,128)} %copy-done.6) | copy-start | bytes 3932164
  579.4 83.3 %copy-start.5 = (f32[1,5,64,4,256]{4,3,2,1,0:T(4,128)S(1)}, f32[1,5,64,4,256]{4,3,2,1,0:T(4,128)}, u32[]{:S(2)}) copy-start(f32[1,5,64,4,256]{4,3,2,1,0:T(4,128)} %param.10) | copy-start | bytes 3932164
  665.7 1.9 copy-start.46
  (19 other events, 26.4 us)
where the time goes:
time: 684 us; the launch traced here: 674 us
  local copies, waits for them, and re-layouts  243 us (36%)
  blocking collectives  130 us (19%)
  starting transfers between devices  111 us (16%)
  other arithmetic  66.6 us (10%)
  matrix products  62.5 us (9%)
  waiting for transfers between devices  49.4 us (7%)
  between operations  12 us (2%)
    psum x2, blocking collectives, body(): lax.psum((local_projection, local_energy), ('tm', 'col'))  130 us
    slice x2, local copies, waits for them, and re-layouts, body(): adjoint = adjoint_step(adjoint, wind_field[moment], mixer) + inject[moment]  48.9 us
    all_to_all x2, starting transfers between devices, body(): lax.all_to_all(picked.reshape(owners, capacity, profile), 'col', split_ax...  45.6 us
    gather x2, local copies, waits for them, and re-layouts, body(): picked = flat_history[slot_ids, :, cell_ids] * filled  41.9 us
    another operation x15, local copies, waits for them, and re-layouts, forward_steps(): return (jnp.stack(slot_states), values)  36.8 us
    unnamed x123, local copies, waits for them, and re-layouts  36.8 us
    dot_general x8, matrix products, adjoint_step(): jnp.einsum('flk,flyx->fkyx', mixer, values, precision=lax.Precision.HIGHEST)  30.9 us
    dot_general x8, matrix products, apply_mix(): jnp.einsum('fkl,flyx->fkyx', mixer, values, precision=lax.Precision.HIGHEST)  24.1 us
  transfers between devices with their start and end apart: 25, of which 5 were waited for; matrix products, arithmetic and copies ran while one was open for 43% of the time, Pallas kernels for 0%

commit v1 on v0

v1 whole, which is shorter than its diff:
```python
import functools

import jax
import jax.numpy as jnp
from jax import lax
from jax.experimental import pallas as pl
from jax.experimental.pallas import tpu as pltpu
from jax.sharding import PartitionSpec as P

F32, BF16, I32 = jnp.float32, jnp.bfloat16, jnp.int32
MESH = pl.DeviceIdType.MESH
LEVELS, LAT, WIDTH, STEPS, CHANNELS = 64, 4, 256, 4, 128
ROWS, INST = 512, 4
INST_ROWS = ROWS // INST
SLOTS = 2 * ROWS
CELLS = LAT * WIDTH
HALO = 16
GROUPS = ((0, 4), (4, 4), (8, 2))


def split2(x):
    hi = x.astype(BF16)
    return hi, (x - hi.astype(F32)).astype(BF16)


def pack(w):
    row = jnp.concatenate(split2(w), axis=1)
    return jnp.concatenate([row, row], axis=0)


def halves(o):
    return o[:, :128] + o[:, 128:]


def mm(u, w):
    left = jnp.concatenate(split2(u), axis=1)
    return halves(jnp.dot(left, w, preferred_element_type=F32))


def native_rows(block, y, xt, count):
    return pl.ds(block * LEVELS * 2 * LAT + xt * LAT + y, count, stride=2 * LAT)


def load_pair(ref, g, y, xt):
    return ref[native_rows(2 * g, y, xt, 128), :]


def load_last(ref, y, xt):
    top = ref[native_rows(4, y, xt, 64), :]
    low = ref[native_rows(4, y + 2, xt, 64), :]
    return jnp.concatenate([top, low], axis=0)


def folded(x):
    return jnp.sum(x.reshape(x.shape[0] // 8, 8, 128), axis=0)


def system_kernel(
    n, nt,
    f_in, d_in, c_in, vm, jac, inn, rvar, col, slot, cnt,
    v1n, v2n, pun, pm_out, sc_out,
    f_t, df_t, rf, rd, c_t, v1, closing, arr, z, yacc, ysplit, rowsplit, keyrow,
    wa, wf, jf, jt, p_mat, pt_mat,
    send_m, send_1, send_2, recv_m, recv_1, recv_2, obs_s, obs_r,
    acc, red, redbuf, zred, zbuf,
    a2a_ss, a2a_rs, z_ss, z_rs, h_ss, h_rs, vh_ss, vh_rs, zz_ss, zz_rs,
):
    cap = SLOTS // n
    s, c = lax.axis_index("tm"), lax.axis_index("col")
    prev_s, next_s = lax.rem(s + nt - 1, nt), lax.rem(s + 1, nt)
    west, east = lax.rem(c + n - 1, n), lax.rem(c + 1, n)

    def rcopy(src, dst, ss, rs, to):
        return pltpu.make_async_remote_copy(
            src_ref=src, dst_ref=dst, send_sem=ss, recv_sem=rs, device_id=to, device_id_type=MESH
        )

    barrier = pltpu.get_barrier_semaphore()

    def greet(to):
        pl.semaphore_signal(barrier, inc=1, device_id=to, device_id_type=MESH)

    greet((prev_s, west))
    greet((next_s, east))

    @pl.loop(1, nt)
    def _(d):
        greet((lax.rem(s + d, nt), c))

    @pl.loop(1, n)
    def _(d):
        greet((s, lax.rem(c + d, n)))

    @pl.loop(0, 8)
    def _(k):
        for xt in range(2):
            f_t[k, pl.ds(xt * 128, 128), :] = load_pair(f_in, k // 4, k % 4, xt).T

    @pl.loop(0, 2)
    def _(y):
        for xt in range(2):
            f_t[8 + y, pl.ds(xt * 128, 128), :] = load_last(f_in, y, xt).T

    pl.semaphore_wait(barrier, n + nt)

    def z_send(src, dst, base, to):
        rest = []
        for i, (k0, kn) in enumerate(GROUPS):
            rest.append(
                rcopy(
                    src.at[pl.ds(k0, kn)], dst.at[pl.ds(k0, kn), pl.ds(0, WIDTH)],
                    z_ss.at[base + i], z_rs.at[base + i], to,
                )
            )
        return rest

    def z_halo(src, dst, i):
        return rcopy(
            src.at[:, pl.ds(0, HALO)], dst.at[:, pl.ds(WIDTH, HALO)],
            h_ss.at[i], h_rs.at[i], (prev_s, west),
        )

    f_halo = z_halo(f_t, rf, 0)
    f_halo.start()
    f_send = z_send(f_t, rf, 0, (prev_s, c))
    for copy in f_send:
        copy.start()

    rows_iota = lax.broadcasted_iota(I32, (ROWS, ROWS), 0)
    lane_iota = lax.broadcasted_iota(I32, (ROWS, ROWS), 1)
    upper_ones = jnp.where(rows_iota <= lane_iota, 1.0, 0.0).astype(BF16)
    column = col[...]
    shift_w, mask_n = WIDTH.bit_length() - 1, n - 1
    owner = (column >> shift_w) & mask_n
    cell = (column >> (shift_w + n.bit_length() - 1)) * WIDTH + (column & (WIDTH - 1))
    key = (slot[...] * CELLS + cell).astype(F32)
    owners = lax.broadcasted_iota(I32, (n, ROWS), 0)
    owned = jnp.where(owners == owner, 1.0, 0.0)
    ranks = jnp.dot(owned.astype(BF16), upper_ones, preferred_element_type=F32)
    landing = jnp.sum(owned * ((owners * cap).astype(F32) + ranks - 1.0), axis=0, keepdims=True)

    def as_column(row, b):
        return jnp.broadcast_to(row[:, b * 128:(b + 1) * 128], (128, 128)).T

    key_col = jnp.concatenate([as_column(key, b) for b in range(4)], axis=0)
    for b in range(SLOTS // 128):
        spots = (lax.broadcasted_iota(I32, (128, ROWS), 0) + b * 128).astype(F32)
        p_mat[b * 128:(b + 1) * 128, :] = jnp.where(spots == landing, 1.0, 0.0).astype(BF16)
    spots = lax.broadcasted_iota(I32, (128, SLOTS), 1).astype(F32)
    for b in range(ROWS // 128):
        land_col = jnp.concatenate([as_column(landing, b)] * (SLOTS // 128), axis=1)
        pt_mat[b * 128:(b + 1) * 128, :] = jnp.where(spots == land_col, 1.0, 0.0).astype(BF16)

    def placed(parts, out):
        right = jnp.concatenate(parts, axis=1)
        for b in range(4):
            o = jnp.dot(p_mat[b * 256:(b + 1) * 256, :], right, preferred_element_type=F32)
            total = o[:, :128]
            for i in range(1, len(parts)):
                total = total + o[:, i * 128:(i + 1) * 128]
            out[b * 256:(b + 1) * 256, :] = total

    def split3(x):
        hi, rest = x.astype(BF16), x - x.astype(BF16).astype(F32)
        return (hi,) + split2(rest)

    def exchange(i, src, dst, d):
        peer = lax.rem(c + d, n)
        return rcopy(
            src.at[pl.ds(pl.multiple_of(peer * cap, cap), cap)],
            dst.at[pl.ds(pl.multiple_of(c * cap, cap), cap)],
            a2a_ss.at[i, d], a2a_rs.at[i, d], (s, peer),
        )

    def exchange_start(i, src, dst):
        @pl.loop(1, n)
        def _(d):
            exchange(i, src, dst, d).start()

        mine = pl.ds(pl.multiple_of(c * cap, cap), cap)
        dst[mine, :] = src[mine, :]

    def exchange_wait(i, src, dst):
        @pl.loop(1, n)
        def _(d):
            peer = lax.rem(c + n - d, n)
            rcopy(
                src.at[pl.ds(0, cap)],
                dst.at[pl.ds(pl.multiple_of(peer * cap, cap), cap)],
                a2a_ss.at[i, d], a2a_rs.at[i, d], (s, peer),
            ).wait_recv()

    def exchange_sent(i, src, dst):
        @pl.loop(1, n)
        def _(d):
            exchange(i, src, dst, d).wait_send()

    placed(split2(key_col), send_m)
    exchange_start(0, send_m, recv_m)
    inst_iota = lax.broadcasted_iota(I32, (INST_ROWS, CHANNELS), 0)
    weight = jnp.concatenate(
        [jnp.where(inst_iota < cnt[0, i], 1.0, 0.0) for i in range(INST)], axis=0
    )
    wd = weight * inn[...]
    placed(split3(wd), send_1)
    exchange_start(1, send_1, recv_1)

    acc[...] = jnp.zeros_like(acc)

    def wind(m, y, xt):
        return c_in[native_rows(m, y, xt, 64), :]

    @pl.loop(0, STEPS * LAT)
    def _(i):
        m, y = i // LAT, i % LAT
        for xt in range(2):
            one = wind(m, y, xt)
            c_t[m * 6 + y, pl.ds(HALO + xt * 128, 128), :] = jnp.concatenate([one, one], axis=0).T

    @pl.loop(0, STEPS * 2)
    def _(i):
        m, y = i // 2, i % 2
        for xt in range(2):
            both = jnp.concatenate([wind(m, y, xt), wind(m, y + 2, xt)], axis=0)
            c_t[m * 6 + 4 + y, pl.ds(HALO + xt * 128, 128), :] = both.T

    c_west = rcopy(
        c_t.at[:, pl.ds(HALO, HALO)], c_t.at[:, pl.ds(HALO + WIDTH, HALO)],
        h_ss.at[2], h_rs.at[2], (s, west),
    )
    c_east = rcopy(
        c_t.at[:, pl.ds(WIDTH, HALO)], c_t.at[:, pl.ds(0, HALO)],
        h_ss.at[3], h_rs.at[3], (s, east),
    )
    c_west.start()
    c_east.start()

    eye = jnp.where(
        lax.broadcasted_iota(I32, (64, 64), 0) == lax.broadcasted_iota(I32, (64, 64), 1), 1.0, 0.0
    )
    nothing = jnp.zeros((64, 64), F32)
    for g, (fa, fb) in enumerate(((0, 1), (2, 3), (4, 4))):
        ma, mb = 0.6 * eye + 0.4 * vm[fa], 0.6 * eye + 0.4 * vm[fb]
        block = jnp.concatenate(
            [jnp.concatenate([ma, nothing], axis=1), jnp.concatenate([nothing, mb], axis=1)],
            axis=0,
        )
        wa[g] = pack(block)
        wf[g] = pack(block.T)
    none = jnp.zeros((64, CHANNELS), F32)
    last = jac[256:320, :]
    for g, block in enumerate(
        (
            jac[0:128, :], jac[128:256, :],
            jnp.concatenate([last, none], axis=0), jnp.concatenate([none, last], axis=0),
        )
    ):
        jf[g] = pack(block)
        jt[g] = pack(block.T)

    @pl.loop(0, 8)
    def _(k):
        for xt in range(2):
            g, y = k // 4, k % 4
            df_t[k, pl.ds(xt * 128, 128), :] = (
                load_pair(f_in, g, y, xt) * load_pair(d_in, g, y, xt)
            ).T

    @pl.loop(0, 2)
    def _(y):
        for xt in range(2):
            df_t[8 + y, pl.ds(xt * 128, 128), :] = (
                load_last(f_in, y, xt) * load_last(d_in, y, xt)
            ).T

    d_halo = z_halo(df_t, rd, 1)
    d_halo.start()
    d_send = z_send(df_t, rd, 3, (prev_s, c))
    for copy in d_send:
        copy.start()

    wrd = weight * (rvar[...] * wd)
    placed(split3(wrd), send_2)
    exchange_start(2, send_2, recv_2)

    def scatter(r, rows):
        rowsplit[...] = jnp.concatenate(split2(rows[...]), axis=1)

        @pl.loop(0, STEPS * LAT)
        def _(i):
            spot = (lax.broadcasted_iota(I32, (WIDTH, SLOTS), 0) + i * WIDTH).astype(F32)
            hit = jnp.where(spot == keyrow[0:1, :], 1.0, 0.0).astype(BF16)
            o = jnp.dot(hit, rowsplit[...], preferred_element_type=F32)
            z[r, i, pl.ds(0, WIDTH), :] = halves(o)

        edge = rcopy(
            z.at[r, :, pl.ds(0, HALO)], z.at[r, :, pl.ds(WIDTH, HALO)],
            h_ss.at[4 + r], h_rs.at[4 + r], (s, west),
        )
        edge.start()
        return edge

    exchange_wait(0, send_m, recv_m)
    for b in range(SLOTS // 128):
        keyrow[:, b * 128:(b + 1) * 128] = recv_m[b * 128:(b + 1) * 128, :].T[0:8, :]
    exchange_wait(1, send_1, recv_1)
    z_edge1 = scatter(0, recv_1)

    later = jnp.where(s < nt - 1, -1.0, 0.0).astype(F32)
    span = WIDTH + HALO

    def adjoint(r, k, g, wind_at, inject, received, own):
        a = received[k] * later
        for m in reversed(range(STEPS)):
            w = mm(a, wa[g])
            p = c_t[m * 6 + wind_at, pl.ds(HALO, span), :] * w
            a = w - p + pltpu.roll(p, span - 1, 0) + inject(m)
        return own[k] + a[0:WIDTH, :]

    def adjoint_pair(r, k, received, own):
        g, y = k // 4, k % 4
        return adjoint(r, k, g, y, lambda m: mm(z[r, m * LAT + y], jt[g]), received, own)

    def adjoint_last(r, y, received, own):
        def inject(m):
            return mm(z[r, m * LAT + y], jt[2]) + mm(z[r, m * LAT + y + 2], jt[3])

        return adjoint(r, 8 + y, 2, 4 + y, inject, received, own)

    def forward(k, g, wind_at, observe):
        v = v1[k]
        for m in range(STEPS):
            observe(m, v[HALO:, :])
            wind_now = c_t[m * 6 + wind_at, pl.ds(0, span), :]
            v = mm(v - wind_now * (v - pltpu.roll(v, 1, 0)), wf[g])
        closing[k] = v[HALO:, :]

    def put_pair(ref, g, y, value):
        for xt in range(2):
            ref[native_rows(2 * g, y, xt, 128), :] = value[xt * 128:(xt + 1) * 128, :].T

    def put_last(ref, y, value):
        for xt in range(2):
            turned = value[xt * 128:(xt + 1) * 128, :].T
            ref[native_rows(4, y, xt, 64), :] = turned[:64, :]
            ref[native_rows(4, y + 2, xt, 64), :] = turned[64:, :]

    yacc[...] = jnp.zeros_like(yacc)
    c_west.wait_recv()
    c_east.wait_recv()
    f_halo.wait_recv()
    z_edge1.wait_recv()

    def edge_v1(i):
        k0, kn = GROUPS[i]
        return rcopy(
            v1.at[pl.ds(k0, kn), pl.ds(WIDTH, HALO)], v1.at[pl.ds(k0, kn), pl.ds(0, HALO)],
            vh_ss.at[i], vh_rs.at[i], (s, east),
        )

    def send_closing(i):
        k0, kn = GROUPS[i]
        return rcopy(
            closing.at[pl.ds(k0, kn)], arr.at[pl.ds(k0, kn)],
            zz_ss.at[i], zz_rs.at[i], (next_s, c),
        )

    edges = [edge_v1(i) for i in range(3)]
    closings = [send_closing(i) for i in range(3)]

    def first_adjoint(i):
        f_send[i].wait_recv()
        if i < 2:
            @pl.loop(4 * i, 4 * i + 4)
            def _(k):
                value = adjoint_pair(0, k, rf, f_t)
                v1[k, pl.ds(HALO, WIDTH), :] = value
                acc[1] += folded(value * value)
                put_pair(v1n, k // 4, k % 4, value)
        else:
            @pl.loop(0, 2)
            def _(y):
                value = adjoint_last(0, y, rf, f_t)
                v1[8 + y, pl.ds(HALO, WIDTH), :] = value
                acc[1] += folded(value * value)
                put_last(v1n, y, value)
        edges[i].start()

    def first_forward(i):
        edges[i].wait_recv()
        if i < 2:
            @pl.loop(4 * i, 4 * i + 4)
            def _(k):
                g, y = k // 4, k % 4

                def observe(m, v):
                    yacc[m * LAT + y] += mm(v, jf[g])

                forward(k, g, y, observe)
        else:
            @pl.loop(0, 2)
            def _(y):
                def observe(m, v):
                    yacc[m * LAT + y] += mm(v, jf[2])
                    yacc[m * LAT + y + 2] += mm(v, jf[3])

                forward(8 + y, 2, 4 + y, observe)
        closings[i].start()

    first_adjoint(0)
    exchange_wait(2, send_2, recv_2)
    z_edge2 = scatter(1, recv_2)
    first_forward(0)
    first_adjoint(1)
    first_forward(1)
    first_adjoint(2)
    first_forward(2)

    @pl.loop(0, STEPS * LAT)
    def _(i):
        ysplit[pl.ds(pl.multiple_of(i * WIDTH, WIDTH), WIDTH), :] = jnp.concatenate(
            split2(yacc[i]), axis=1
        )

    @pl.loop(0, 4)
    def _(b):
        rows = pl.ds(pl.multiple_of(b * 256, 256), 256)
        at = jnp.concatenate([recv_m[rows, :]] * (CELLS // 128), axis=1)
        total = jnp.zeros((256, 256), F32)
        for m in range(STEPS):
            spot = (lax.broadcasted_iota(I32, (256, CELLS), 1) + m * CELLS).astype(F32)
            hit = jnp.where(spot == at, 1.0, 0.0).astype(BF16)
            total = total + jnp.dot(
                hit, ysplit[m * CELLS:(m + 1) * CELLS, :], preferred_element_type=F32
            )
        obs_s[rows, :] = halves(total)

    exchange_start(3, obs_s, obs_r)

    @pl.loop(0, 10)
    def _(i):
        rows = pl.ds(pl.multiple_of(i * 256, 256), 256)
        f = f_in[rows, :]
        df = f * d_in[rows, :]
        acc[0] += folded(f * df)
        acc[1] += folded(df * df)

    acc[0] += folded(wd * wrd)
    acc[1] += folded(wrd * wrd)

    d_halo.wait_recv()
    z_edge2.wait_recv()

    def second_adjoint(i):
        d_send[i].wait_recv()

        def take(k, value):
            own = v1[k, pl.ds(HALO, WIDTH), :]
            acc[3] += folded(own * value)
            acc[4] += folded(value * value)

        if i < 2:
            @pl.loop(4 * i, 4 * i + 4)
            def _(k):
                value = adjoint_pair(1, k, rd, df_t)
                take(k, value)
                put_pair(v2n, k // 4, k % 4, value)
        else:
            @pl.loop(0, 2)
            def _(y):
                value = adjoint_last(1, y, rd, df_t)
                take(8 + y, value)
                put_last(v2n, y, value)

    has_before = jnp.where(s > 0, 1.0, 0.0).astype(F32)

    def arrive(i):
        closings[i].wait_recv()
        if i < 2:
            @pl.loop(4 * i, 4 * i + 4)
            def _(k):
                value = v1[k, pl.ds(HALO, WIDTH), :] - has_before * arr[k]
                put_pair(pun, k // 4, k % 4, value)
        else:
            @pl.loop(0, 2)
            def _(y):
                value = v1[8 + y, pl.ds(HALO, WIDTH), :] - has_before * arr[8 + y]
                put_last(pun, y, value)

    second_adjoint(0)
    second_adjoint(1)
    for i in range(3):
        arrive(i)

    @pl.loop(0, 10)
    def _(i):
        rows = pl.ds(pl.multiple_of(i * 256, 256), 256)
        f, d = f_in[rows, :], d_in[rows, :]
        df = f * d
        pu = d * df + pun[rows, :]
        pun[rows, :] = pu
        acc[2] += folded(f * pu)
        acc[3] += folded(df * pu)
        acc[4] += folded(pu * pu)

    exchange_wait(3, obs_s, obs_r)
    right = jnp.concatenate(split2(obs_r[...]), axis=1)
    seen = halves(jnp.dot(pt_mat[...], right, preferred_element_type=F32))
    pm = weight * (rvar[...] * wrd + seen)
    pm_out[...] = pm
    acc[2] += folded(wd * pm)
    acc[3] += folded(wrd * pm)
    acc[4] += folded(pm * pm)

    second_adjoint(2)

    lines = [jnp.sum(acc[i], axis=0, keepdims=True) for i in range(5)]
    red[...] = jnp.concatenate(lines + [jnp.zeros((3, 128), F32)], axis=0)

    def share(d):
        return rcopy(
            red, redbuf.at[c], a2a_ss.at[4, d], a2a_rs.at[4, d], (s, lax.rem(c + d, n))
        )

    @pl.loop(1, n)
    def _(d):
        share(d).start()

    redbuf[c] = red[...]

    @pl.loop(1, n)
    def _(d):
        peer = lax.rem(c + n - d, n)
        rcopy(red, redbuf.at[peer], a2a_ss.at[4, d], a2a_rs.at[4, d], (s, peer)).wait_recv()

    zred[...] = jnp.sum(redbuf[...], axis=0)

    def share_z(d):
        return rcopy(
            zred, zbuf.at[s], z_ss.at[6 + d], z_rs.at[6 + d], (lax.rem(s + d, nt), c)
        )

    for d in range(1, nt):
        share_z(d).start()
    zbuf[s] = zred[...]
    for d in range(1, nt):
        peer = lax.rem(s + nt - d, nt)
        rcopy(zred, zbuf.at[peer], z_ss.at[6 + d], z_rs.at[6 + d], (peer, c)).wait_recv()

    total = jnp.sum(jnp.sum(zbuf[...], axis=0), axis=1, keepdims=True)
    total = jnp.broadcast_to(total, (8, 128))
    rq, qq, rp, qp, pp = (total[i:i + 1, :] for i in range(5))
    step1 = rq / qq
    step2 = step1 * (step1 * qp - rp) / (qq - 2.0 * step1 * qp + step1 * step1 * pp)
    sc_out[...] = jnp.concatenate(
        [step1 + step2, step1 * step2, jnp.zeros((6, 128), F32)], axis=0
    )

    for i, (src, dst) in enumerate(
        ((send_m, recv_m), (send_1, recv_1), (send_2, recv_2), (obs_s, obs_r))
    ):
        exchange_sent(i, src, dst)

    @pl.loop(1, n)
    def _(d):
        share(d).wait_send()

    for d in range(1, nt):
        share_z(d).wait_send()
    for copy in [f_halo, d_halo, c_west, c_east, z_edge1, z_edge2] + f_send + d_send:
        copy.wait_send()
    for copy in edges + closings:
        copy.wait_send()


def finish_kernel(sc, f_in, d_in, v1, v2, pu, inn, rvar, cnt, pm, ms, rs, xs, mr, rr, xr):
    t, q = sc[0:1, :], sc[1:2, :]
    f, d = f_in[...], d_in[...]
    df = f * d
    ms[...] = t * f - q * df
    mr[...] = f - t * df + q * pu[...]
    v = v1[...]
    xs[...] = -(q * v)
    xr[...] = q * v2[...] - t * v
    inside = lax.broadcasted_iota(I32, (INST_ROWS, CHANNELS), 0) < cnt[0, pl.program_id(0)]
    weight = jnp.where(inside, 1.0, 0.0)
    wd = weight * inn[...]
    wrd = weight * (rvar[...] * wd)
    rs[...] = t * wd - q * wrd
    rr[...] = wd - t * wrd + q * pm[...]


def to_rows(x):
    a, b, y, w = x.shape
    return x.reshape(a, b, y, w // 128, 128).transpose(0, 1, 3, 2, 4).reshape(-1, 128)


def from_rows(x, shape):
    a, b, y, w = shape
    return x.reshape(a, b, w // 128, y, 128).transpose(0, 1, 3, 2, 4).reshape(shape)


def body(n, nt, forcing_state, model_error, courant, vertical_mix, radiance_jacobian,
         innovation, report_error, report_column, report_slot, report_count):
    f, d, wind = (to_rows(x[0]) for x in (forcing_state, model_error, courant))
    inn, rvar, cnt = innovation[0], report_error[0], report_count[0]
    size = f.shape[0]
    vmem = pl.BlockSpec(memory_space=pltpu.VMEM)
    smem = pl.BlockSpec(memory_space=pltpu.SMEM)
    V = pltpu.VMEM
    state = jax.ShapeDtypeStruct((size, 128), F32)
    reports = jax.ShapeDtypeStruct((ROWS, CHANNELS), F32)
    span = WIDTH + HALO
    slots = V((SLOTS, 128), F32)
    dma = pltpu.SemaphoreType.DMA
    v1, v2, pu, pm, sc = pl.pallas_call(
        functools.partial(system_kernel, n, nt),
        out_shape=(state, state, state, reports, jax.ShapeDtypeStruct((8, 128), F32)),
        in_specs=[vmem] * 9 + [smem],
        out_specs=(vmem,) * 5,
        scratch_shapes=[
            V((10, WIDTH, 128), F32), V((10, WIDTH, 128), F32),
            V((10, span, 128), F32), V((10, span, 128), F32),
            V((6 * STEPS, span + HALO, 128), F32),
            V((10, span, 128), F32), V((10, WIDTH, 128), F32), V((10, WIDTH, 128), F32),
            V((2, STEPS * LAT, span, 128), F32), V((STEPS * LAT, WIDTH, 128), F32),
            V((STEPS * CELLS, 256), BF16), V((SLOTS, 256), BF16), V((8, SLOTS), F32),
            V((3, 256, 256), BF16), V((3, 256, 256), BF16),
            V((4, 256, 256), BF16), V((4, 256, 256), BF16),
            V((SLOTS, ROWS), BF16), V((ROWS, SLOTS), BF16),
            slots, slots, slots, slots, slots, slots, slots, slots,
            V((5, 8, 128), F32), V((8, 128), F32), V((n, 8, 128), F32),
            V((8, 128), F32), V((nt, 8, 128), F32),
            dma((5, n)), dma((5, n)), dma((6 + nt,)), dma((6 + nt,)),
            dma((6,)), dma((6,)), dma((3,)), dma((3,)), dma((3,)), dma((3,)),
        ],
        compiler_params=pltpu.CompilerParams(
            collective_id=0, has_side_effects=True, vmem_limit_bytes=56 * 1024 * 1024
        ),
        cost_estimate=pl.CostEstimate(flops=40 * 10**9, bytes_accessed=10**7, transcendentals=0),
    )(f, d, wind, vertical_mix, radiance_jacobian, inn, rvar, report_column, report_slot, cnt)
    part = pl.BlockSpec((size // INST, 128), lambda i: (i, 0))
    rpart = pl.BlockSpec((INST_ROWS, CHANNELS), lambda i: (i, 0))
    ms, rs, xs, mr, rr, xr = pl.pallas_call(
        finish_kernel,
        grid=(INST,),
        out_shape=(state, reports, state, state, reports, state),
        in_specs=[
            pl.BlockSpec((8, 128), lambda i: (0, 0)), part, part, part, part, part,
            rpart, rpart, smem, rpart,
        ],
        out_specs=(part, rpart, part, part, rpart, part),
        compiler_params=pltpu.CompilerParams(vmem_limit_bytes=32 * 1024 * 1024),
    )(sc, f, d, v1, v2, pu, inn, rvar, cnt, pm)
    shape = forcing_state.shape[1:]
    ms, xs, mr, xr = (from_rows(x, shape)[None] for x in (ms, xs, mr, xr))
    return ms, rs[None], xs, mr, rr[None], xr


def solution(mesh):
    grid = P("tm", None, None, None, "col")
    reports = P("tm", "col", None)
    in_specs = (
        grid, grid, grid, P(), P(), reports, reports, P("tm", "col"), P("tm", "col"), reports,
    )
    out_specs = (grid, reports, grid, grid, reports, grid)
    run = functools.partial(body, mesh.shape["col"], mesh.shape["tm"])
    return jax.shard_map(run, mesh=mesh, in_specs=in_specs, out_specs=out_specs, check_vma=False)
```

time: 684 us -> 106 us (0.15); the launches traced: 674 us -> 106 us
  local copies, waits for them, and re-layouts: 243 us -> 5.58 us
  blocking collectives: 130 us -> 0 us
  starting transfers between devices: 111 us -> 0 us
  Pallas kernels: 0 us -> 99.2 us
  other arithmetic: 66.6 us -> 0 us
  matrix products: 62.5 us -> 0 us
  waiting for transfers between devices: 49.4 us -> 0 us
  between operations: 12 us -> 0.74 us
    psum x2 -> x0, blocking collectives: 130 us -> none  [body(): lax.psum((local_projection, local_energy), ('tm', 'col'))]
    pallas_call x0 -> x2, Pallas kernels: none -> 99.2 us  [the longest x1 95.8 us: body(): pl.pallas_call(functools.partial(system_kernel, n, nt), out_shape=(state,...]
    slice x41 -> x0, local copies, waits for them, and re-layouts: 73.5 us -> none  [the longest x2 48.9 us: body(): adjoint = adjoint_step(adjoint, wind_field[moment], mixer) + inject[moment]]
    all_to_all x5 -> x0, starting transfers between devices: 68.1 us -> none  [the longest x2 45.6 us: body(): lax.all_to_all(picked.reshape(owners, capacity, profile), 'col', split_ax...]
    dot_general x20 -> x0, matrix products: 62.5 us -> none  [the longest x8 30.9 us: adjoint_step(): jnp.einsum('flk,flyx->fkyx', mixer, values, precision=lax.Precision.HIGHEST)]
    gather x4 -> x0, local copies, waits for them, and re-layouts: 46.5 us -> none  [the longest x2 41.9 us: body(): picked = flat_history[slot_ids, :, cell_ids] * filled]
    ppermute x20 -> x0, starting transfers between devices: 42.7 us -> none  [the longest x4 22.2 us: from_behind(): lax.ppermute(value, axis, [(source, source + steps) for source in range(i...]
    another operation x18 -> x0, local copies, waits for them, and re-layouts: 37.2 us -> none  [the longest x15 36.8 us: forward_steps(): return (jnp.stack(slot_states), values)]
  transfers between devices with their start and end apart: 25 -> 0, of which waited for: 5 -> 0; matrix products, arithmetic and copies ran while one was open for 43% -> 0% of each run, Pallas kernels for 0% -> 0%
where the time goes in v1:
time: 106 us
  Pallas kernels  99.2 us (94%)
  local copies, waits for them, and re-layouts  5.58 us (5%)
    pallas_call x1, Pallas kernels, body(): pl.pallas_call(functools.partial(system_kernel, n, nt), out_shape=(state,...  95.8 us
    unnamed x20, local copies, waits for them, and re-layouts  5.58 us
    pallas_call x1, Pallas kernels, body(): pl.pallas_call(finish_kernel, grid=(INST,), out_shape=(state, reports, st...  3.44 us

profile of v1, /device:TPU:1, one launch (start us, length us, event | category | flops | bytes accessed | tf_op | source)
XLA Modules:
  0.0 105.5 jit_solution(12410755045780414202)
XLA Ops:
  0.6 0.0 copy-start
  0.6 0.0 copy-start.1
  0.7 0.0 copy-start.5
  0.7 0.0 copy-start.6
  0.7 0.0 copy-start.9
  0.7 95.8 %shard_map.145 = (f32[2560,128]{1,0:T(8,128)}, f32[2560,128]{1,0:T(8,128)}, f32[2560,128]{1,0:T(8,128)}, f32[512,128]{1,0:T(8,128)}, f32[8,128]{1,0:T(8,128)}) custom-call(f32[2560,128]{1,0:T(8,128)} %bitcast.40, f32[2560,128]{1,0:T(8,128)} %bitcast.42, f32[2048,128]{1,0:T(8,128)} %bitcast.54, f32[5,64,64]{2,1,0:T(8,128)} %vm.1, f32[320,128]{1,0:T(8,128)} %jac.1, ...), custom_call_target="tpu_custom_call" | custom-call | flops 40000000000 | bytes 10000000 | tf_op jit(solution)/shard_map/pallas_call | solution.py:616
  96.5 0.0 copy-done
  96.5 0.0 copy-done.1
  96.5 0.0 copy-done.5
  96.5 0.0 copy-done.6
  96.5 0.0 copy-done.9
  96.5 0.0 copy-start.2
  96.5 1.3 %copy-done.2 = f32[2560,128]{1,0:T(8,128)S(1)} copy-done((f32[2560,128]{1,0:T(8,128)S(1)}, f32[2560,128]{1,0:T(8,128)}, u32[]{:S(2)}) %copy-start.2) | copy-done | bytes 1310744
  97.8 0.0 copy-start.3
  97.8 1.3 %copy-done.3 = f32[2560,128]{1,0:T(8,128)S(1)} copy-done((f32[2560,128]{1,0:T(8,128)S(1)}, f32[2560,128]{1,0:T(8,128)}, u32[]{:S(2)}) %copy-start.3) | copy-done | bytes 1310744
  99.2 0.0 copy-start.4
  99.2 1.3 %copy-done.4 = f32[2560,128]{1,0:T(8,128)S(1)} copy-done((f32[2560,128]{1,0:T(8,128)S(1)}, f32[2560,128]{1,0:T(8,128)}, u32[]{:S(2)}) %copy-start.4) | copy-done | bytes 1310744
  100.5 0.0 copy-start.7
  100.5 0.9 copy-done.7
  101.4 0.0 copy-start.8
  101.4 0.7 copy-done.8
  102.1 3.4 %shard_map.146 = (f32[2560,128]{1,0:T(8,128)}, f32[512,128]{1,0:T(8,128)}, f32[2560,128]{1,0:T(8,128)}, f32[2560,128]{1,0:T(8,128)}, f32[512,128]{1,0:T(8,128)}, /*index=5*/f32[2560,128]{1,0:T(8,128)}) custom-call(f32[8,128]{1,0:T(8,128)S(1)} %copy-done.8, f32[2560,128]{1,0:T(8,128)S(1)} %bitcast.41, f32[2560,128]{1,0:T(8,128)S(1)} %bitcast.43, ...), custom_call_target="tpu_custom_call" | custom-call | tf_op jit(solution)/shard_map/pallas_call | solution.py:644
Async XLA Ops:
  0.6 95.8 %copy-start = (f32[1,5,64,4,256]{4,3,2,1,0:T(4,128)S(1)}, f32[1,5,64,4,256]{4,3,2,1,0:T(4,128)}, u32[]{:S(2)}) copy-start(f32[1,5,64,4,256]{4,3,2,1,0:T(4,128)} %param.10) | copy-start | bytes 3932164
  0.6 95.8 %copy-start.1 = (f32[1,5,64,4,256]{4,3,2,1,0:T(4,128)S(1)}, f32[1,5,64,4,256]{4,3,2,1,0:T(4,128)}, u32[]{:S(2)}) copy-start(f32[1,5,64,4,256]{4,3,2,1,0:T(4,128)} %param.11) | copy-start | bytes 3932164
  0.7 95.8 %copy-start.5 = (f32[1,512,128]{2,1,0:T(8,128)S(1)}, f32[1,512,128]{2,1,0:T(8,128)}, u32[]{:S(2)}) copy-start(f32[1,512,128]{2,1,0:T(8,128)} %param.15) | copy-start | bytes 786436
  0.7 95.8 %copy-start.6 = (f32[1,512,128]{2,1,0:T(8,128)S(1)}, f32[1,512,128]{2,1,0:T(8,128)}, u32[]{:S(2)}) copy-start(f32[1,512,128]{2,1,0:T(8,128)} %param.16) | copy-start | bytes 786436
  0.7 95.8 %copy-start.9 = (s32[1,1,4]{2,1,0:T(1,128)S(1)}, s32[1,1,4]{2,1,0:T(1,128)}, u32[]{:S(2)}) copy-start(s32[1,1,4]{2,1,0:T(1,128)} %param.19) | copy-start | bytes 52
  96.5 1.3 %copy-start.2 = (f32[2560,128]{1,0:T(8,128)S(1)}, f32[2560,128]{1,0:T(8,128)}, u32[]{:S(2)}) copy-start(f32[2560,128]{1,0:T(8,128)} %get-tuple-element.18.v1) | copy-start | bytes 3932164
  97.8 1.3 %copy-start.3 = (f32[2560,128]{1,0:T(8,128)S(1)}, f32[2560,128]{1,0:T(8,128)}, u32[]{:S(2)}) copy-start(f32[2560,128]{1,0:T(8,128)} %get-tuple-element.19.v2) | copy-start | bytes 3932164
  99.2 1.3 %copy-start.4 = (f32[2560,128]{1,0:T(8,128)S(1)}, f32[2560,128]{1,0:T(8,128)}, u32[]{:S(2)}) copy-start(f32[2560,128]{1,0:T(8,128)} %get-tuple-element.20.pu) | copy-start | bytes 3932164
  100.5 0.9 copy-start.7
  101.4 0.7 copy-start.8

commit v2 on v1

v2 whole, which is shorter than its diff:
```python
import functools

import jax
import jax.numpy as jnp
from jax import lax
from jax.experimental import pallas as pl
from jax.experimental.pallas import tpu as pltpu
from jax.sharding import PartitionSpec as P

F32, BF16, I32 = jnp.float32, jnp.bfloat16, jnp.int32
MESH = pl.DeviceIdType.MESH
LEVELS, LAT, WIDTH, STEPS, CHANNELS = 64, 4, 256, 4, 128
ROWS, INST = 512, 4
INST_ROWS = ROWS // INST
SLOTS = 2 * ROWS
CELLS = LAT * WIDTH
HALO, EDGE = 16, 8
LAST = 8
GROUPS = ((0, 4), (4, 4), (8, 2))


def split2(x):
    hi = x.astype(BF16)
    return hi, (x - hi.astype(F32)).astype(BF16)


def pack(w):
    row = jnp.concatenate(split2(w), axis=1)
    return jnp.concatenate([row, row], axis=0)


def halves(o):
    return o[:, :128] + o[:, 128:]


def mm(u, w):
    left = jnp.concatenate(split2(u), axis=1)
    return halves(jnp.dot(left, w, preferred_element_type=F32))


def native_rows(block, y, xt, count):
    return pl.ds(block * LEVELS * 2 * LAT + xt * LAT + y, count, stride=2 * LAT)


def load_pair(ref, g, y, xt):
    return ref[native_rows(2 * g, y, xt, 128), :]


def load_last(ref, y, xt):
    top = ref[native_rows(4, y, xt, 64), :]
    low = ref[native_rows(4, y + 2, xt, 64), :]
    return jnp.concatenate([top, low], axis=0)


def folded(x):
    return jnp.sum(x.reshape(x.shape[0] // 8, 8, 128), axis=0)


def system_kernel(
    n, nt,
    f_hbm, d_hbm, c_hbm, vm_hbm, jac_hbm, inn_hbm, rvar_hbm, col_hbm, slot_hbm, cnt_hbm,
    f_in, d_in, v1n, v2n, pun, wd_out, wrd_out, pm_out, sc_out,
    c_in, vm, jac, inn, rvar, col, slot, cnt,
    f_t, df_t, rf, rd, c_t, v1, closing, arr, z, yacc, ysplit, rowsplit, keyrow,
    wa, wf, jf, jt, p_mat, pt_mat, send_a, recv_a, obs_s, obs_r,
    acc, red, redbuf, zred, zbuf,
    in_s, a2a_ss, a2a_rs, z_ss, z_rs, h_ss, h_rs, vh_ss, vh_rs, zz_ss, zz_rs,
):
    cap = SLOTS // n
    s, c = lax.axis_index("tm"), lax.axis_index("col")
    prev_s, next_s = lax.rem(s + nt - 1, nt), lax.rem(s + 1, nt)
    west, east = lax.rem(c + n - 1, n), lax.rem(c + 1, n)

    def rcopy(src, dst, ss, rs, to):
        return pltpu.make_async_remote_copy(
            src_ref=src, dst_ref=dst, send_sem=ss, recv_sem=rs, device_id=to, device_id_type=MESH
        )

    pairs = (
        (f_hbm, f_in), (col_hbm, col), (slot_hbm, slot), (cnt_hbm, cnt), (inn_hbm, inn),
        (rvar_hbm, rvar), (c_hbm, c_in), (vm_hbm, vm), (jac_hbm, jac), (d_hbm, d_in),
    )
    loads = [pltpu.make_async_copy(a, b, in_s.at[i]) for i, (a, b) in enumerate(pairs)]
    for load in loads:
        load.start()

    barrier = pltpu.get_barrier_semaphore()

    def greet(to):
        pl.semaphore_signal(barrier, inc=1, device_id=to, device_id_type=MESH)

    greet((prev_s, west))
    greet((next_s, east))

    @pl.loop(1, nt)
    def _(d):
        greet((lax.rem(s + d, nt), c))

    @pl.loop(1, n)
    def _(d):
        greet((s, lax.rem(c + d, n)))

    loads[0].wait()

    @pl.loop(0, 8)
    def _(k):
        for xt in range(2):
            f_t[k, pl.ds(xt * 128, 128), :] = load_pair(f_in, k // 4, k % 4, xt).T

    @pl.loop(0, 2)
    def _(y):
        for xt in range(2):
            f_t[8 + y, pl.ds(xt * 128, 128), :] = load_last(f_in, y, xt).T

    pl.semaphore_wait(barrier, n + nt)

    def z_send(src, dst, base, to):
        rest = []
        for i, (k0, kn) in enumerate(GROUPS):
            rest.append(
                rcopy(
                    src.at[pl.ds(k0, kn)], dst.at[pl.ds(k0, kn), pl.ds(0, WIDTH)],
                    z_ss.at[base + i], z_rs.at[base + i], to,
                )
            )
        return rest

    def z_halo(src, dst, i):
        return rcopy(
            src.at[:, pl.ds(0, EDGE)], dst.at[:, pl.ds(WIDTH, EDGE)],
            h_ss.at[i], h_rs.at[i], (prev_s, west),
        )

    f_halo = z_halo(f_t, rf, 0)
    f_halo.start()
    f_send = z_send(f_t, rf, 0, (prev_s, c))
    for copy in f_send:
        copy.start()

    rows_iota = lax.broadcasted_iota(I32, (ROWS, ROWS), 0)
    lane_iota = lax.broadcasted_iota(I32, (ROWS, ROWS), 1)
    upper_ones = jnp.where(rows_iota <= lane_iota, 1.0, 0.0).astype(BF16)
    for load in loads[1:4]:
        load.wait()
    column = col[...]
    shift_w, mask_n = WIDTH.bit_length() - 1, n - 1
    owner = (column >> shift_w) & mask_n
    cell = (column >> (shift_w + n.bit_length() - 1)) * WIDTH + (column & (WIDTH - 1))
    key = (slot[...] * CELLS + cell).astype(F32)
    owners = lax.broadcasted_iota(I32, (n, ROWS), 0)
    owned = jnp.where(owners == owner, 1.0, 0.0)
    ranks = jnp.dot(owned.astype(BF16), upper_ones, preferred_element_type=F32)
    landing = jnp.sum(owned * ((owners * cap).astype(F32) + ranks - 1.0), axis=0, keepdims=True)

    def as_column(row, b):
        return jnp.broadcast_to(row[:, b * 128:(b + 1) * 128], (128, 128)).T

    key_col = jnp.concatenate([as_column(key, b) for b in range(4)], axis=0)
    for b in range(SLOTS // 128):
        spots = (lax.broadcasted_iota(I32, (128, ROWS), 0) + b * 128).astype(F32)
        p_mat[b * 128:(b + 1) * 128, :] = jnp.where(spots == landing, 1.0, 0.0).astype(BF16)
    spots = lax.broadcasted_iota(I32, (128, SLOTS), 1).astype(F32)
    for b in range(ROWS // 128):
        land_col = jnp.concatenate([as_column(landing, b)] * (SLOTS // 128), axis=1)
        pt_mat[b * 128:(b + 1) * 128, :] = jnp.where(spots == land_col, 1.0, 0.0).astype(BF16)

    def split3(x):
        hi, rest = x.astype(BF16), x - x.astype(BF16).astype(F32)
        return (hi,) + split2(rest)

    def exchange(i, src, dst, d):
        peer = lax.rem(c + d, n)
        return rcopy(
            src.at[peer], dst.at[c], a2a_ss.at[i, d], a2a_rs.at[i, d], (s, peer)
        )

    def exchange_start(i, src, dst):
        @pl.loop(1, n)
        def _(d):
            exchange(i, src, dst, d).start()

        dst[c] = src[c]

    def exchange_wait(i, src, dst):
        @pl.loop(1, n)
        def _(d):
            peer = lax.rem(c + n - d, n)
            rcopy(
                src.at[peer], dst.at[peer], a2a_ss.at[i, d], a2a_rs.at[i, d], (s, peer)
            ).wait_recv()

    def exchange_sent(i, src, dst):
        @pl.loop(1, n)
        def _(d):
            exchange(i, src, dst, d).wait_send()

    loads[4].wait()
    loads[5].wait()
    inst_iota = lax.broadcasted_iota(I32, (INST_ROWS, CHANNELS), 0)
    weight = jnp.concatenate(
        [jnp.where(inst_iota < cnt[0:1, i:i + 1], 1.0, 0.0) for i in range(INST)], axis=0
    )
    wd = weight * inn[...]
    wrd = weight * (rvar[...] * wd)
    wd_out[...] = wd
    wrd_out[...] = wrd
    parts = split3(wd) + split3(wrd) + split2(key_col)
    right = jnp.concatenate(parts, axis=1)
    per = 256 // cap
    for b in range(4):
        o = jnp.dot(p_mat[b * 256:(b + 1) * 256, :], right, preferred_element_type=F32)
        o = [o[:, i * 128:(i + 1) * 128] for i in range(8)]
        for i, total in enumerate((o[0] + o[1] + o[2], o[3] + o[4] + o[5], o[6] + o[7])):
            send_a[b * per:(b + 1) * per, i * cap:(i + 1) * cap, :] = total.reshape(per, cap, 128)
    exchange_start(0, send_a, recv_a)

    acc[...] = jnp.zeros_like(acc)

    loads[6].wait()

    def wind(m, y, xt):
        return c_in[native_rows(m, y, xt, 64), :]

    @pl.loop(0, STEPS * LAT)
    def _(i):
        m, y = i // LAT, i % LAT
        for xt in range(2):
            one = wind(m, y, xt)
            c_t[m * 6 + y, pl.ds(HALO + xt * 128, 128), :] = jnp.concatenate([one, one], axis=0).T

    @pl.loop(0, STEPS * 2)
    def _(i):
        m, y = i // 2, i % 2
        for xt in range(2):
            both = jnp.concatenate([wind(m, y, xt), wind(m, y + 2, xt)], axis=0)
            c_t[m * 6 + 4 + y, pl.ds(HALO + xt * 128, 128), :] = both.T

    c_west = rcopy(
        c_t.at[:, pl.ds(HALO, EDGE)], c_t.at[:, pl.ds(HALO + WIDTH, EDGE)],
        h_ss.at[2], h_rs.at[2], (s, west),
    )
    c_east = rcopy(
        c_t.at[:, pl.ds(WIDTH + HALO - EDGE, EDGE)], c_t.at[:, pl.ds(HALO - EDGE, EDGE)],
        h_ss.at[3], h_rs.at[3], (s, east),
    )
    c_west.start()
    c_east.start()

    loads[7].wait()
    loads[8].wait()

    eye = jnp.where(
        lax.broadcasted_iota(I32, (64, 64), 0) == lax.broadcasted_iota(I32, (64, 64), 1), 1.0, 0.0
    )
    nothing = jnp.zeros((64, 64), F32)
    for g, (fa, fb) in enumerate(((0, 1), (2, 3), (4, 4))):
        ma, mb = 0.6 * eye + 0.4 * vm[fa], 0.6 * eye + 0.4 * vm[fb]
        block = jnp.concatenate(
            [jnp.concatenate([ma, nothing], axis=1), jnp.concatenate([nothing, mb], axis=1)],
            axis=0,
        )
        wa[g] = pack(block)
        wf[g] = pack(block.T)
    none = jnp.zeros((64, CHANNELS), F32)
    last = jac[256:320, :]
    for g, block in enumerate(
        (
            jac[0:128, :], jac[128:256, :],
            jnp.concatenate([last, none], axis=0), jnp.concatenate([none, last], axis=0),
        )
    ):
        jf[g] = pack(block)
        jt[g] = pack(block.T)

    loads[9].wait()

    @pl.loop(0, 8)
    def _(k):
        for xt in range(2):
            g, y = k // 4, k % 4
            df_t[k, pl.ds(xt * 128, 128), :] = (
                load_pair(f_in, g, y, xt) * load_pair(d_in, g, y, xt)
            ).T

    @pl.loop(0, 2)
    def _(y):
        for xt in range(2):
            df_t[8 + y, pl.ds(xt * 128, 128), :] = (
                load_last(f_in, y, xt) * load_last(d_in, y, xt)
            ).T

    d_halo = z_halo(df_t, rd, 1)
    d_halo.start()
    d_send = z_send(df_t, rd, 3, (prev_s, c))
    for copy in d_send:
        copy.start()

    exchange_wait(0, send_a, recv_a)

    def received_rows(i):
        return recv_a[:, i * cap:(i + 1) * cap, :].reshape(SLOTS, 128)

    keys = received_rows(2)
    for b in range(SLOTS // 128):
        keyrow[:, b * 128:(b + 1) * 128] = keys[b * 128:(b + 1) * 128, :].T[0:8, :]
    rowsplit[...] = jnp.concatenate(split2(received_rows(0)) + split2(received_rows(1)), axis=1)

    @pl.loop(0, STEPS * LAT)
    def _(i):
        spot = (lax.broadcasted_iota(I32, (WIDTH, SLOTS), 0) + i * WIDTH).astype(F32)
        hit = jnp.where(spot == keyrow[0:1, :], 1.0, 0.0).astype(BF16)
        o = jnp.dot(hit, rowsplit[...], preferred_element_type=F32)
        z[0, i, pl.ds(0, WIDTH), :] = halves(o[:, :256])
        z[1, i, pl.ds(0, WIDTH), :] = halves(o[:, 256:])

    z_edge = rcopy(
        z.at[:, pl.ds(LAT, 3 * LAT), pl.ds(0, EDGE)],
        z.at[:, pl.ds(LAT, 3 * LAT), pl.ds(WIDTH, EDGE)],
        h_ss.at[4], h_rs.at[4], (s, west),
    )
    z_edge.start()

    later = jnp.where(s < nt - 1, -1.0, 0.0).astype(F32)
    span = WIDTH + HALO

    def block(x, first, rows, count):
        return x[pl.ds(first, 2), pl.ds(rows, count), :].reshape(2 * count, 128)

    def adjoint(r, k, g, y, received, own):
        a = block(received, k, 0, span) * later
        wind_at = 4 if k is LAST else y
        for m in reversed(range(STEPS)):
            w = mm(a, wa[g])
            p = block(c_t, m * 6 + wind_at, HALO, span) * w
            if k is LAST:
                inject = mm(block(z.at[r], m * LAT, 0, span), jt[2])
                inject = inject + mm(block(z.at[r], m * LAT + 2, 0, span), jt[3])
            else:
                inject = mm(block(z.at[r], m * LAT + y, 0, span), jt[g])
            a = w - p + pltpu.roll(p, 2 * span - 1, 0) + inject
        a = a.reshape(2, span, 128)
        return [own[k + i] + a[i, 0:WIDTH, :] for i in range(2)]

    def forward(k, g, y):
        v = block(v1, k, 0, span)
        wind_at = 4 if k is LAST else y
        for m in range(STEPS):
            inner = v.reshape(2, span, 128)[:, HALO:, :].reshape(2 * WIDTH, 128)
            if k is LAST:
                yacc[pl.ds(m * LAT, 2)] += mm(inner, jf[2]).reshape(2, WIDTH, 128)
                yacc[pl.ds(m * LAT + 2, 2)] += mm(inner, jf[3]).reshape(2, WIDTH, 128)
            else:
                yacc[pl.ds(m * LAT + y, 2)] += mm(inner, jf[g]).reshape(2, WIDTH, 128)
            wind_now = block(c_t, m * 6 + wind_at, 0, span)
            v = mm(v - wind_now * (v - pltpu.roll(v, 1, 0)), wf[g])
        closing[pl.ds(k, 2)] = v.reshape(2, span, 128)[:, HALO:, :]

    def each_pair(i, run):
        if i < 2:
            @pl.loop(0, 2)
            def _(j):
                run(4 * i + 2 * j, i, 2 * j)
        else:
            run(LAST, 2, 0)

    def put_pair(ref, g, y, value):
        for xt in range(2):
            ref[native_rows(2 * g, y, xt, 128), :] = value[xt * 128:(xt + 1) * 128, :].T

    def put(ref, k, g, y, value):
        if g == 2:
            put_last(ref, y, value)
        else:
            put_pair(ref, g, y, value)

    def put_last(ref, y, value):
        for xt in range(2):
            turned = value[xt * 128:(xt + 1) * 128, :].T
            ref[native_rows(4, y, xt, 64), :] = turned[:64, :]
            ref[native_rows(4, y + 2, xt, 64), :] = turned[64:, :]

    yacc[...] = jnp.zeros_like(yacc)
    c_west.wait_recv()
    c_east.wait_recv()
    f_halo.wait_recv()
    z_edge.wait_recv()

    def edge_v1(i):
        k0, kn = GROUPS[i]
        return rcopy(
            v1.at[pl.ds(k0, kn), pl.ds(WIDTH + HALO - EDGE, EDGE)],
            v1.at[pl.ds(k0, kn), pl.ds(HALO - EDGE, EDGE)],
            vh_ss.at[i], vh_rs.at[i], (s, east),
        )

    def send_closing(i):
        k0, kn = GROUPS[i]
        return rcopy(
            closing.at[pl.ds(k0, kn)], arr.at[pl.ds(k0, kn)],
            zz_ss.at[i], zz_rs.at[i], (next_s, c),
        )

    edges = [edge_v1(i) for i in range(3)]
    closings = [send_closing(i) for i in range(3)]

    def first_adjoint(i):
        f_send[i].wait_recv()

        def run(k, g, y):
            for j, value in enumerate(adjoint(0, k, g, y, rf, f_t)):
                v1[k + j, pl.ds(HALO, WIDTH), :] = value
                acc[1] += folded(value * value)
                put(v1n, k + j, g, y + j, value)

        each_pair(i, run)
        edges[i].start()

    def first_forward(i):
        edges[i].wait_recv()
        each_pair(i, forward)
        closings[i].start()

    first_adjoint(0)
    first_adjoint(1)
    first_forward(0)
    first_adjoint(2)
    first_forward(1)
    first_forward(2)

    @pl.loop(0, STEPS * LAT)
    def _(i):
        ysplit[pl.ds(pl.multiple_of(i * WIDTH, WIDTH), WIDTH), :] = jnp.concatenate(
            split2(yacc[i]), axis=1
        )

    @pl.loop(0, 4)
    def _(b):
        took = recv_a[pl.ds(pl.multiple_of(b * per, per), per), 2 * cap:3 * cap, :]
        at = jnp.concatenate([took.reshape(256, 128)] * (CELLS // 128), axis=1)
        total = jnp.zeros((256, 256), F32)
        for m in range(STEPS):
            spot = (lax.broadcasted_iota(I32, (256, CELLS), 1) + m * CELLS).astype(F32)
            hit = jnp.where(spot == at, 1.0, 0.0).astype(BF16)
            total = total + jnp.dot(
                hit, ysplit[m * CELLS:(m + 1) * CELLS, :], preferred_element_type=F32
            )
        obs_s[pl.ds(pl.multiple_of(b * per, per), per)] = halves(total).reshape(per, cap, 128)

    exchange_start(1, obs_s, obs_r)

    @pl.loop(0, 10)
    def _(i):
        rows = pl.ds(pl.multiple_of(i * 256, 256), 256)
        f = f_in[rows, :]
        df = f * d_in[rows, :]
        acc[0] += folded(f * df)
        acc[1] += folded(df * df)

    acc[0] += folded(wd * wrd)
    acc[1] += folded(wrd * wrd)

    d_halo.wait_recv()

    def second_adjoint(i):
        d_send[i].wait_recv()

        def run(k, g, y):
            for j, value in enumerate(adjoint(1, k, g, y, rd, df_t)):
                own = v1[k + j, pl.ds(HALO, WIDTH), :]
                acc[3] += folded(own * value)
                acc[4] += folded(value * value)
                put(v2n, k + j, g, y + j, value)

        each_pair(i, run)

    has_before = jnp.where(s > 0, 1.0, 0.0).astype(F32)

    def arrive(i):
        closings[i].wait_recv()
        def run(k, g, y):
            for j in range(2):
                value = v1[k + j, pl.ds(HALO, WIDTH), :] - has_before * arr[k + j]
                put(pun, k + j, g, y + j, value)

        each_pair(i, run)

    second_adjoint(0)
    second_adjoint(1)
    for i in range(3):
        arrive(i)

    @pl.loop(0, 10)
    def _(i):
        rows = pl.ds(pl.multiple_of(i * 256, 256), 256)
        f, d = f_in[rows, :], d_in[rows, :]
        df = f * d
        pu = d * df + pun[rows, :]
        pun[rows, :] = pu
        acc[2] += folded(f * pu)
        acc[3] += folded(df * pu)
        acc[4] += folded(pu * pu)

    exchange_wait(1, obs_s, obs_r)
    right = jnp.concatenate(split2(obs_r[...].reshape(SLOTS, 128)), axis=1)
    seen = halves(jnp.dot(pt_mat[...], right, preferred_element_type=F32))
    pm = weight * (rvar[...] * wrd + seen)
    pm_out[...] = pm
    acc[2] += folded(wd * pm)
    acc[3] += folded(wrd * pm)
    acc[4] += folded(pm * pm)

    second_adjoint(2)

    lines = [jnp.sum(acc[i], axis=0, keepdims=True) for i in range(5)]
    red[...] = jnp.concatenate(lines + [jnp.zeros((3, 128), F32)], axis=0)

    def share(d):
        return rcopy(
            red, redbuf.at[c], a2a_ss.at[2, d], a2a_rs.at[2, d], (s, lax.rem(c + d, n))
        )

    @pl.loop(1, n)
    def _(d):
        share(d).start()

    redbuf[c] = red[...]

    @pl.loop(1, n)
    def _(d):
        peer = lax.rem(c + n - d, n)
        rcopy(red, redbuf.at[peer], a2a_ss.at[2, d], a2a_rs.at[2, d], (s, peer)).wait_recv()

    zred[...] = jnp.sum(redbuf[...], axis=0)

    def share_z(d):
        return rcopy(
            zred, zbuf.at[s], z_ss.at[6 + d], z_rs.at[6 + d], (lax.rem(s + d, nt), c)
        )

    for d in range(1, nt):
        share_z(d).start()
    zbuf[s] = zred[...]
    for d in range(1, nt):
        peer = lax.rem(s + nt - d, nt)
        rcopy(zred, zbuf.at[peer], z_ss.at[6 + d], z_rs.at[6 + d], (peer, c)).wait_recv()

    total = jnp.sum(jnp.sum(zbuf[...], axis=0), axis=1, keepdims=True)
    total = jnp.broadcast_to(total, (8, 128))
    rq, qq, rp, qp, pp = (total[i:i + 1, :] for i in range(5))
    step1 = rq / qq
    step2 = step1 * (step1 * qp - rp) / (qq - 2.0 * step1 * qp + step1 * step1 * pp)
    sc_out[...] = jnp.concatenate(
        [step1 + step2, step1 * step2, jnp.zeros((6, 128), F32)], axis=0
    )

    for i, (src, dst) in enumerate(((send_a, recv_a), (obs_s, obs_r))):
        exchange_sent(i, src, dst)

    @pl.loop(1, n)
    def _(d):
        share(d).wait_send()

    for d in range(1, nt):
        share_z(d).wait_send()
    for copy in [f_halo, d_halo, c_west, c_east, z_edge] + f_send + d_send:
        copy.wait_send()
    for copy in edges + closings:
        copy.wait_send()


def finish_kernel(sc, f_in, d_in, v1, v2, pu, wd_in, wrd_in, pm, ms, rs, xs, mr, rr, xr):
    t, q = sc[0:1, :], sc[1:2, :]
    f, d = f_in[...], d_in[...]
    df = f * d
    ms[...] = t * f - q * df
    mr[...] = f - t * df + q * pu[...]
    v = v1[...]
    xs[...] = -(q * v)
    xr[...] = q * v2[...] - t * v
    wd, wrd = wd_in[...], wrd_in[...]
    rs[...] = t * wd - q * wrd
    rr[...] = wd - t * wrd + q * pm[...]


def to_rows(x):
    a, b, y, w = x.shape
    return x.reshape(a, b, y, w // 128, 128).transpose(0, 1, 3, 2, 4).reshape(-1, 128)


def from_rows(x, shape):
    a, b, y, w = shape
    return x.reshape(a, b, w // 128, y, 128).transpose(0, 1, 3, 2, 4).reshape(shape)


def body(n, nt, forcing_state, model_error, courant, vertical_mix, radiance_jacobian,
         innovation, report_error, report_column, report_slot, report_count):
    f, d, wind = (to_rows(x[0]) for x in (forcing_state, model_error, courant))
    inn, rvar, cnt = innovation[0], report_error[0], report_count[0]
    size = f.shape[0]
    vmem = pl.BlockSpec(memory_space=pltpu.VMEM)
    hbm = pl.BlockSpec(memory_space=pltpu.HBM)
    V = pltpu.VMEM
    state = jax.ShapeDtypeStruct((size, 128), F32)
    reports = jax.ShapeDtypeStruct((ROWS, CHANNELS), F32)
    span, cap = WIDTH + HALO, SLOTS // n
    dma = pltpu.SemaphoreType.DMA
    inputs = (
        f, d, wind, vertical_mix, radiance_jacobian, inn, rvar, report_column, report_slot, cnt,
    )
    inputs = tuple(pltpu.with_memory_space_constraint(x, pltpu.HBM) for x in inputs)
    results = pl.pallas_call(
        functools.partial(system_kernel, n, nt),
        out_shape=(state,) * 5 + (reports,) * 3 + (jax.ShapeDtypeStruct((8, 128), F32),),
        in_specs=[hbm] * 10,
        out_specs=(vmem,) * 9,
        scratch_shapes=[V(x.shape, x.dtype) for x in inputs[2:]] + [
            V((10, WIDTH, 128), F32), V((10, WIDTH, 128), F32),
            V((10, span, 128), F32), V((10, span, 128), F32),
            V((6 * STEPS, span + HALO, 128), F32),
            V((10, span, 128), F32), V((10, WIDTH, 128), F32), V((10, WIDTH, 128), F32),
            V((2, STEPS * LAT, span, 128), F32), V((STEPS * LAT, WIDTH, 128), F32),
            V((STEPS * CELLS, 256), BF16), V((SLOTS, 512), BF16), V((8, SLOTS), F32),
            V((3, 256, 256), BF16), V((3, 256, 256), BF16),
            V((4, 256, 256), BF16), V((4, 256, 256), BF16),
            V((SLOTS, ROWS), BF16), V((ROWS, SLOTS), BF16),
            V((n, 3 * cap, 128), F32), V((n, 3 * cap, 128), F32),
            V((n, cap, 128), F32), V((n, cap, 128), F32),
            V((5, 8, 128), F32), V((8, 128), F32), V((n, 8, 128), F32),
            V((8, 128), F32), V((nt, 8, 128), F32),
            dma((10,)), dma((3, n)), dma((3, n)), dma((6 + nt,)), dma((6 + nt,)),
            dma((5,)), dma((5,)), dma((3,)), dma((3,)), dma((3,)), dma((3,)),
        ],
        compiler_params=pltpu.CompilerParams(
            collective_id=0, has_side_effects=True, vmem_limit_bytes=42 * 1024 * 1024
        ),
        cost_estimate=pl.CostEstimate(flops=40 * 10**9, bytes_accessed=10**7, transcendentals=0),
    )(*inputs)
    fv, dv, v1, v2, pu, wd, wrd, pm, sc = results
    steps = 8
    part = pl.BlockSpec((size // steps, 128), lambda i: (i, 0))
    rpart = pl.BlockSpec((ROWS // steps, CHANNELS), lambda i: (i, 0))
    ms, rs, xs, mr, rr, xr = pl.pallas_call(
        finish_kernel,
        grid=(steps,),
        out_shape=(state, reports, state, state, reports, state),
        in_specs=[pl.BlockSpec((8, 128), lambda i: (0, 0))] + [part] * 5 + [rpart] * 3,
        out_specs=(part, rpart, part, part, rpart, part),
        compiler_params=pltpu.CompilerParams(vmem_limit_bytes=32 * 1024 * 1024),
    )(sc, fv, dv, v1, v2, pu, wd, wrd, pm)
    shape = forcing_state.shape[1:]
    ms, xs, mr, xr = (from_rows(x, shape)[None] for x in (ms, xs, mr, xr))
    return ms, rs[None], xs, mr, rr[None], xr


def solution(mesh):
    grid = P("tm", None, None, None, "col")
    reports = P("tm", "col", None)
    in_specs = (
        grid, grid, grid, P(), P(), reports, reports, P("tm", "col"), P("tm", "col"), reports,
    )
    out_specs = (grid, reports, grid, grid, reports, grid)
    run = functools.partial(body, mesh.shape["col"], mesh.shape["tm"])
    return jax.shard_map(run, mesh=mesh, in_specs=in_specs, out_specs=out_specs, check_vma=False)
```

time: 106 us -> 106 us (level)
  Pallas kernels: 99.2 us -> 105 us
  local copies, waits for them, and re-layouts: 5.58 us -> 0 us
    unnamed x20 -> x0, local copies, waits for them, and re-layouts: 5.58 us -> none
    pallas_call x1, Pallas kernels: 95.8 us -> 101 us  [body(): pl.pallas_call(functools.partial(system_kernel, n, nt), out_shape=(state,...]
where the time goes in v2:
time: 106 us
  Pallas kernels  105 us (99%)
    pallas_call x1, Pallas kernels, body(): pl.pallas_call(functools.partial(system_kernel, n, nt), out_shape=(state,...  101 us
    pallas_call x1, Pallas kernels, body(): pl.pallas_call(finish_kernel, grid=(steps,), out_shape=(state, reports, s...  3.79 us

profile of v2, /device:TPU:1, one launch (start us, length us, event | category | flops | bytes accessed | tf_op | source)
XLA Modules:
  0.0 105.6 jit_solution(719790060830780004)
XLA Ops:
  0.6 101.1 %shard_map.145 = (f32[2560,128]{1,0:T(8,128)S(1)}, f32[2560,128]{1,0:T(8,128)S(1)}, f32[2560,128]{1,0:T(8,128)S(1)}, f32[2560,128]{1,0:T(8,128)S(1)}, f32[2560,1...) custom-call(f32[2560,128]{1,0:T(8,128)} %bitcast.40, ...), custom_call_target="tpu_custom_call" | custom-call | flops 40000000000 | bytes 10000000 | tf_op jit(solution)/shard_map/pallas_call | solution.py:611
  101.8 3.8 %shard_map.146 = (f32[2560,128]{1,0:T(8,128)}, f32[512,128]{1,0:T(8,128)}, f32[2560,128]{1,0:T(8,128)}, f32[2560,128]{1,0:T(8,128)}, f32[512,128]{1,0:T(8,128)}, /*index=5*/f32[2560,128]{1,0:T(8,128)}) custom-call(f32[8,128]{1,0:T(8,128)S(1)} %get-tuple-element.21.sc, f32[2560,128]{1,0:T(8,128)S(1)} %get-tuple-element.22.f_in, ...), custom_call_target="tpu_custom_call" | custom-call | tf_op jit(solution)/shard_map/pallas_call | solution.py:642

commit v3 on v2

--- a/solution.py
+++ b/solution.py
@@ -61,8 +61,8 @@
     f_hbm, d_hbm, c_hbm, vm_hbm, jac_hbm, inn_hbm, rvar_hbm, col_hbm, slot_hbm, cnt_hbm,
     f_in, d_in, v1n, v2n, pun, wd_out, wrd_out, pm_out, sc_out,
     c_in, vm, jac, inn, rvar, col, slot, cnt,
-    f_t, df_t, rf, rd, c_t, v1, closing, arr, z, yacc, ysplit, rowsplit, keyrow,
-    wa, wf, jf, jt, p_mat, pt_mat, send_a, recv_a, obs_s, obs_r,
+    f_t, df_t, rf, rd, c_t, v1, closing, arr, z, yacc, ysplit, rowsplit, keyrow, keycol,
+    wa, wf, jf, jt, p_mat, pt_mat, send_a, recv_a, send_b, recv_b, obs_s, obs_r,
     acc, red, redbuf, zred, zbuf,
     in_s, a2a_ss, a2a_rs, z_ss, z_rs, h_ss, h_rs, vh_ss, vh_rs, zz_ss, zz_rs,
 ):
@@ -75,44 +75,6 @@
         return pltpu.make_async_remote_copy(
             src_ref=src, dst_ref=dst, send_sem=ss, recv_sem=rs, device_id=to, device_id_type=MESH
         )
-
-    pairs = (
-        (f_hbm, f_in), (col_hbm, col), (slot_hbm, slot), (cnt_hbm, cnt), (inn_hbm, inn),
-        (rvar_hbm, rvar), (c_hbm, c_in), (vm_hbm, vm), (jac_hbm, jac), (d_hbm, d_in),
-    )
-    loads = [pltpu.make_async_copy(a, b, in_s.at[i]) for i, (a, b) in enumerate(pairs)]
-    for load in loads:
-        load.start()
-
-    barrier = pltpu.get_barrier_semaphore()
-
-    def greet(to):
-        pl.semaphore_signal(barrier, inc=1, device_id=to, device_id_type=MESH)
-
-    greet((prev_s, west))
-    greet((next_s, east))
-
-    @pl.loop(1, nt)
-    def _(d):
-        greet((lax.rem(s + d, nt), c))
-
-    @pl.loop(1, n)
-    def _(d):
-        greet((s, lax.rem(c + d, n)))
-
-    loads[0].wait()
-
-    @pl.loop(0, 8)
-    def _(k):
-        for xt in range(2):
-            f_t[k, pl.ds(xt * 128, 128), :] = load_pair(f_in, k // 4, k % 4, xt).T
-
-    @pl.loop(0, 2)
-    def _(y):
-        for xt in range(2):
-            f_t[8 + y, pl.ds(xt * 128, 128), :] = load_last(f_in, y, xt).T
-
-    pl.semaphore_wait(barrier, n + nt)
 
     def z_send(src, dst, base, to):
         rest = []
@@ -131,11 +93,67 @@
             h_ss.at[i], h_rs.at[i], (prev_s, west),
         )
 
-    f_halo = z_halo(f_t, rf, 0)
-    f_halo.start()
-    f_send = z_send(f_t, rf, 0, (prev_s, c))
-    for copy in f_send:
-        copy.start()
+    def exchange(i, src, dst, d):
+        peer = lax.rem(c + d, n)
+        return rcopy(
+            src.at[peer], dst.at[c], a2a_ss.at[i, d], a2a_rs.at[i, d], (s, peer)
+        )
+
+    def exchange_start(i, src, dst):
+        @pl.loop(1, n)
+        def _(d):
+            exchange(i, src, dst, d).start()
+
+        dst[c] = src[c]
+
+    def exchange_wait(i, src, dst):
+        @pl.loop(1, n)
+        def _(d):
+            peer = lax.rem(c + n - d, n)
+            rcopy(
+                src.at[peer], dst.at[peer], a2a_ss.at[i, d], a2a_rs.at[i, d], (s, peer)
+            ).wait_recv()
+
+    def exchange_sent(i, src, dst):
+        @pl.loop(1, n)
+        def _(d):
+            exchange(i, src, dst, d).wait_send()
+
+    pairs = (
+        (f_hbm, f_in), (col_hbm, col), (slot_hbm, slot), (cnt_hbm, cnt), (inn_hbm, inn),
+        (rvar_hbm, rvar), (c_hbm, c_in), (vm_hbm, vm), (jac_hbm, jac), (d_hbm, d_in),
+    )
+    loads = [pltpu.make_async_copy(a, b, in_s.at[i]) for i, (a, b) in enumerate(pairs)]
+    for load in loads:
+        load.start()
+
+    barrier = pltpu.get_barrier_semaphore()
+
+    def greet(to):
+        pl.semaphore_signal(barrier, inc=1, device_id=to, device_id_type=MESH)
+
+    greet((prev_s, west))
+    greet((next_s, east))
+
+    @pl.loop(1, nt)
+    def _(d):
+        greet((lax.rem(s + d, nt), c))
+
+    @pl.loop(1, n)
+    def _(d):
+        greet((s, lax.rem(c + d, n)))
+
+    loads[0].wait()
+
+    @pl.loop(0, 8)
+    def _(k):
+        for xt in range(2):
+            f_t[k, pl.ds(xt * 128, 128), :] = load_pair(f_in, k // 4, k % 4, xt).T
+
+    @pl.loop(0, 2)
+    def _(y):
+        for xt in range(2):
+            f_t[8 + y, pl.ds(xt * 128, 128), :] = load_last(f_in, y, xt).T
 
     rows_iota = lax.broadcasted_iota(I32, (ROWS, ROWS), 0)
     lane_iota = lax.broadcasted_iota(I32, (ROWS, ROWS), 1)
@@ -155,7 +173,6 @@
     def as_column(row, b):
         return jnp.broadcast_to(row[:, b * 128:(b + 1) * 128], (128, 128)).T
 
-    key_col = jnp.concatenate([as_column(key, b) for b in range(4)], axis=0)
     for b in range(SLOTS // 128):
         spots = (lax.broadcasted_iota(I32, (128, ROWS), 0) + b * 128).astype(F32)
         p_mat[b * 128:(b + 1) * 128, :] = jnp.where(spots == landing, 1.0, 0.0).astype(BF16)
@@ -168,32 +185,6 @@
         hi, rest = x.astype(BF16), x - x.astype(BF16).astype(F32)
         return (hi,) + split2(rest)
 
-    def exchange(i, src, dst, d):
-        peer = lax.rem(c + d, n)
-        return rcopy(
-            src.at[peer], dst.at[c], a2a_ss.at[i, d], a2a_rs.at[i, d], (s, peer)
-        )
-
-    def exchange_start(i, src, dst):
-        @pl.loop(1, n)
-        def _(d):
-            exchange(i, src, dst, d).start()
-
-        dst[c] = src[c]
-
-    def exchange_wait(i, src, dst):
-        @pl.loop(1, n)
-        def _(d):
-            peer = lax.rem(c + n - d, n)
-            rcopy(
-                src.at[peer], dst.at[peer], a2a_ss.at[i, d], a2a_rs.at[i, d], (s, peer)
-            ).wait_recv()
-
-    def exchange_sent(i, src, dst):
-        @pl.loop(1, n)
-        def _(d):
-            exchange(i, src, dst, d).wait_send()
-
     loads[4].wait()
     loads[5].wait()
     inst_iota = lax.broadcasted_iota(I32, (INST_ROWS, CHANNELS), 0)
@@ -204,14 +195,29 @@
     wrd = weight * (rvar[...] * wd)
     wd_out[...] = wd
     wrd_out[...] = wrd
-    parts = split3(wd) + split3(wrd) + split2(key_col)
-    right = jnp.concatenate(parts, axis=1)
-    per = 256 // cap
+    right = jnp.concatenate(split3(wd) + split3(wrd), axis=1)
+    per, lots = 256 // cap, 128 // cap
     for b in range(4):
         o = jnp.dot(p_mat[b * 256:(b + 1) * 256, :], right, preferred_element_type=F32)
-        o = [o[:, i * 128:(i + 1) * 128] for i in range(8)]
-        for i, total in enumerate((o[0] + o[1] + o[2], o[3] + o[4] + o[5], o[6] + o[7])):
-            send_a[b * per:(b + 1) * per, i * cap:(i + 1) * cap, :] = total.reshape(per, cap, 128)
+        o = [o[:, i * 128:(i + 1) * 128] for i in range(6)]
+        owners_here = slice(b * per, (b + 1) * per)
+        send_a[owners_here, 8:, :] = (o[0] + o[1] + o[2]).reshape(per, cap, 128)
+        send_b[owners_here, :, :] = (o[3] + o[4] + o[5]).reshape(per, cap, 128)
+    keys = 0.0
+    for part in split2(jnp.broadcast_to(key, (16, ROWS))):
+        keys = keys + lax.dot_general(
+            part, p_mat[...], (((1,), (1,)), ((), ())), preferred_element_type=F32
+        )
+    for o in range(n):
+        b = o // lots
+        send_a[o, 0:8, :] = keys[0:8, b * 128:(b + 1) * 128]
+
+    pl.semaphore_wait(barrier, n + nt)
+    f_halo = z_halo(f_t, rf, 0)
+    f_halo.start()
+    f_send = z_send(f_t, rf, 0, (prev_s, c))
+    for copy in f_send:
+        copy.start()
     exchange_start(0, send_a, recv_a)
 
     acc[...] = jnp.zeros_like(acc)
@@ -245,6 +251,29 @@
     )
     c_west.start()
     c_east.start()
+    exchange_start(3, send_b, recv_b)
+    loads[9].wait()
+
+    @pl.loop(0, 8)
+    def _(k):
+        for xt in range(2):
+            g, y = k // 4, k % 4
+            df_t[k, pl.ds(xt * 128, 128), :] = (
+                load_pair(f_in, g, y, xt) * load_pair(d_in, g, y, xt)
+            ).T
+
+    @pl.loop(0, 2)
+    def _(y):
+        for xt in range(2):
+            df_t[8 + y, pl.ds(xt * 128, 128), :] = (
+                load_last(f_in, y, xt) * load_last(d_in, y, xt)
+            ).T
+
+    d_halo = z_halo(df_t, rd, 1)
+    d_halo.start()
+    d_send = z_send(df_t, rd, 3, (prev_s, c))
+    for copy in d_send:
+        copy.start()
 
     loads[7].wait()
     loads[8].wait()
@@ -272,53 +301,45 @@
         jf[g] = pack(block)
         jt[g] = pack(block.T)
 
-    loads[9].wait()
-
-    @pl.loop(0, 8)
-    def _(k):
-        for xt in range(2):
-            g, y = k // 4, k % 4
-            df_t[k, pl.ds(xt * 128, 128), :] = (
-                load_pair(f_in, g, y, xt) * load_pair(d_in, g, y, xt)
-            ).T
-
-    @pl.loop(0, 2)
-    def _(y):
-        for xt in range(2):
-            df_t[8 + y, pl.ds(xt * 128, 128), :] = (
-                load_last(f_in, y, xt) * load_last(d_in, y, xt)
-            ).T
-
-    d_halo = z_halo(df_t, rd, 1)
-    d_halo.start()
-    d_send = z_send(df_t, rd, 3, (prev_s, c))
-    for copy in d_send:
-        copy.start()
-
     exchange_wait(0, send_a, recv_a)
-
-    def received_rows(i):
-        return recv_a[:, i * cap:(i + 1) * cap, :].reshape(SLOTS, 128)
-
-    keys = received_rows(2)
-    for b in range(SLOTS // 128):
-        keyrow[:, b * 128:(b + 1) * 128] = keys[b * 128:(b + 1) * 128, :].T[0:8, :]
-    rowsplit[...] = jnp.concatenate(split2(received_rows(0)) + split2(received_rows(1)), axis=1)
-
-    @pl.loop(0, STEPS * LAT)
-    def _(i):
-        spot = (lax.broadcasted_iota(I32, (WIDTH, SLOTS), 0) + i * WIDTH).astype(F32)
-        hit = jnp.where(spot == keyrow[0:1, :], 1.0, 0.0).astype(BF16)
-        o = jnp.dot(hit, rowsplit[...], preferred_element_type=F32)
-        z[0, i, pl.ds(0, WIDTH), :] = halves(o[:, :256])
-        z[1, i, pl.ds(0, WIDTH), :] = halves(o[:, 256:])
-
-    z_edge = rcopy(
-        z.at[:, pl.ds(LAT, 3 * LAT), pl.ds(0, EDGE)],
-        z.at[:, pl.ds(LAT, 3 * LAT), pl.ds(WIDTH, EDGE)],
-        h_ss.at[4], h_rs.at[4], (s, west),
-    )
-    z_edge.start()
+    meta = pltpu.roll(recv_a[:, 0, :], lax.rem(128 - cap * lax.rem(c, lots), 128), 1)
+    lane = lax.broadcasted_iota(I32, (n, 128), 1)
+    meta = jnp.where(lane < cap, meta, 0.0)
+    tiled = meta
+    for i in range(1, lots):
+        tiled = tiled + pltpu.roll(meta, cap * i, 1)
+    tiled = jnp.concatenate([tiled] * (SLOTS // 128), axis=1)
+    sender = lax.broadcasted_iota(I32, (n, SLOTS), 0)
+    place = lax.broadcasted_iota(I32, (n, SLOTS), 1)
+    mine = (place >= sender * cap) & (place < sender * cap + cap)
+    keyrow[...] = jnp.broadcast_to(
+        jnp.sum(jnp.where(mine, tiled, 0.0), axis=0, keepdims=True), (8, SLOTS)
+    )
+
+    def scatter(r, rows):
+        rowsplit[...] = jnp.concatenate(split2(rows.reshape(SLOTS, 128)), axis=1)
+
+        @pl.loop(0, STEPS * LAT)
+        def _(i):
+            spot = (lax.broadcasted_iota(I32, (WIDTH, SLOTS), 0) + i * WIDTH).astype(F32)
+            hit = jnp.where(spot == keyrow[0:1, :], 1.0, 0.0).astype(BF16)
+            o = jnp.dot(hit, rowsplit[...], preferred_element_type=F32)
+            z[r, i, pl.ds(0, WIDTH), :] = halves(o)
+
+        edge = rcopy(
+            z.at[r, pl.ds(LAT, 3 * LAT), pl.ds(0, EDGE)],
+            z.at[r, pl.ds(LAT, 3 * LAT), pl.ds(WIDTH, EDGE)],
+            h_ss.at[4 + r], h_rs.at[4 + r], (s, west),
+        )
+        edge.start()
+        return edge
+
+    z_edge1 = scatter(0, recv_a[:, 8:, :])
+
+    @pl.loop(0, SLOTS // 128)
+    def _(b):
+        lanes = pl.ds(pl.multiple_of(b * 128, 128), 128)
+        keycol[lanes, :] = jnp.broadcast_to(keyrow[0:1, lanes], (128, 128)).T
 
     later = jnp.where(s < nt - 1, -1.0, 0.0).astype(F32)
     span = WIDTH + HALO
@@ -383,7 +404,7 @@
     c_west.wait_recv()
     c_east.wait_recv()
     f_halo.wait_recv()
-    z_edge.wait_recv()
+    z_edge1.wait_recv()
 
     def edge_v1(i):
         k0, kn = GROUPS[i]
@@ -421,10 +442,24 @@
         closings[i].start()
 
     first_adjoint(0)
+    exchange_wait(3, send_b, recv_b)
+    z_edge2 = scatter(1, recv_b[...])
+    first_forward(0)
     first_adjoint(1)
-    first_forward(0)
+
+    @pl.loop(0, 10)
+    def _(i):
+        rows = pl.ds(pl.multiple_of(i * 256, 256), 256)
+        f = f_in[rows, :]
+        df = f * d_in[rows, :]
+        acc[0] += folded(f * df)
+        acc[1] += folded(df * df)
+
+    acc[0] += folded(wd * wrd)
+    acc[1] += folded(wrd * wrd)
+
+    first_forward(1)
     first_adjoint(2)
-    first_forward(1)
     first_forward(2)
 
     @pl.loop(0, STEPS * LAT)
@@ -435,8 +470,8 @@
 
     @pl.loop(0, 4)
     def _(b):
-        took = recv_a[pl.ds(pl.multiple_of(b * per, per), per), 2 * cap:3 * cap, :]
-        at = jnp.concatenate([took.reshape(256, 128)] * (CELLS // 128), axis=1)
+        took = keycol[pl.ds(pl.multiple_of(b * 256, 256), 256), :]
+        at = jnp.concatenate([took] * (CELLS // 128), axis=1)
         total = jnp.zeros((256, 256), F32)
         for m in range(STEPS):
             spot = (lax.broadcasted_iota(I32, (256, CELLS), 1) + m * CELLS).astype(F32)
@@ -448,18 +483,8 @@
 
     exchange_start(1, obs_s, obs_r)
 
-    @pl.loop(0, 10)
-    def _(i):
-        rows = pl.ds(pl.multiple_of(i * 256, 256), 256)
-        f = f_in[rows, :]
-        df = f * d_in[rows, :]
-        acc[0] += folded(f * df)
-        acc[1] += folded(df * df)
-
-    acc[0] += folded(wd * wrd)
-    acc[1] += folded(wrd * wrd)
-
     d_halo.wait_recv()
+    z_edge2.wait_recv()
 
     def second_adjoint(i):
         d_send[i].wait_recv()
@@ -484,22 +509,26 @@
 
         each_pair(i, run)
 
+    def upper(i):
+        first, count = ((0, 4), (4, 4), (8, 2))[i]
+
+        @pl.loop(first, first + count)
+        def _(b):
+            rows = pl.ds(pl.multiple_of(b * 256, 256), 256)
+            f, d = f_in[rows, :], d_in[rows, :]
+            df = f * d
+            pu = d * df + pun[rows, :]
+            pun[rows, :] = pu
+            acc[2] += folded(f * pu)
+            acc[3] += folded(df * pu)
+            acc[4] += folded(pu * pu)
+
+    arrive(0)
+    upper(0)
     second_adjoint(0)
+    arrive(1)
+    upper(1)
     second_adjoint(1)
-    for i in range(3):
-        arrive(i)
-
-    @pl.loop(0, 10)
-    def _(i):
-        rows = pl.ds(pl.multiple_of(i * 256, 256), 256)
-        f, d = f_in[rows, :], d_in[rows, :]
-        df = f * d
-        pu = d * df + pun[rows, :]
-        pun[rows, :] = pu
-        acc[2] += folded(f * pu)
-        acc[3] += folded(df * pu)
-        acc[4] += folded(pu * pu)
-
     exchange_wait(1, obs_s, obs_r)
     right = jnp.concatenate(split2(obs_r[...].reshape(SLOTS, 128)), axis=1)
     seen = halves(jnp.dot(pt_mat[...], right, preferred_element_type=F32))
@@ -509,6 +538,8 @@
     acc[3] += folded(wrd * pm)
     acc[4] += folded(pm * pm)
 
+    arrive(2)
+    upper(2)
     second_adjoint(2)
 
     lines = [jnp.sum(acc[i], axis=0, keepdims=True) for i in range(5)]
@@ -553,7 +584,7 @@
         [step1 + step2, step1 * step2, jnp.zeros((6, 128), F32)], axis=0
     )
 
-    for i, (src, dst) in enumerate(((send_a, recv_a), (obs_s, obs_r))):
+    for i, src, dst in ((0, send_a, recv_a), (1, obs_s, obs_r), (3, send_b, recv_b)):
         exchange_sent(i, src, dst)
 
     @pl.loop(1, n)
@@ -562,7 +593,7 @@
 
     for d in range(1, nt):
         share_z(d).wait_send()
-    for copy in [f_halo, d_halo, c_west, c_east, z_edge] + f_send + d_send:
+    for copy in [f_halo, d_halo, c_west, c_east, z_edge1, z_edge2] + f_send + d_send:
         copy.wait_send()
     for copy in edges + closings:
         copy.wait_send()
@@ -619,16 +650,17 @@
             V((6 * STEPS, span + HALO, 128), F32),
             V((10, span, 128), F32), V((10, WIDTH, 128), F32), V((10, WIDTH, 128), F32),
             V((2, STEPS * LAT, span, 128), F32), V((STEPS * LAT, WIDTH, 128), F32),
-            V((STEPS * CELLS, 256), BF16), V((SLOTS, 512), BF16), V((8, SLOTS), F32),
+            V((STEPS * CELLS, 256), BF16), V((SLOTS, 256), BF16), V((8, SLOTS), F32), V((SLOTS, 128), F32),
             V((3, 256, 256), BF16), V((3, 256, 256), BF16),
             V((4, 256, 256), BF16), V((4, 256, 256), BF16),
             V((SLOTS, ROWS), BF16), V((ROWS, SLOTS), BF16),
-            V((n, 3 * cap, 128), F32), V((n, 3 * cap, 128), F32),
+            V((n, 8 + cap, 128), F32), V((n, 8 + cap, 128), F32),
+            V((n, cap, 128), F32), V((n, cap, 128), F32),
             V((n, cap, 128), F32), V((n, cap, 128), F32),
             V((5, 8, 128), F32), V((8, 128), F32), V((n, 8, 128), F32),
             V((8, 128), F32), V((nt, 8, 128), F32),
-            dma((10,)), dma((3, n)), dma((3, n)), dma((6 + nt,)), dma((6 + nt,)),
-            dma((5,)), dma((5,)), dma((3,)), dma((3,)), dma((3,)), dma((3,)),
+            dma((10,)), dma((4, n)), dma((4, n)), dma((6 + nt,)), dma((6 + nt,)),
+            dma((6,)), dma((6,)), dma((3,)), dma((3,)), dma((3,)), dma((3,)),
         ],
         compiler_params=pltpu.CompilerParams(
             collective_id=0, has_side_effects=True, vmem_limit_bytes=42 * 1024 * 1024

time: 106 us -> 88.1 us (0.83)
  Pallas kernels: 105 us -> 87.3 us
    pallas_call x1, Pallas kernels: 101 us -> 83.5 us  [body(): pl.pallas_call(functools.partial(system_kernel, n, nt), out_shape=(state,...]
where the time goes in v3:
time: 88.1 us; the launch traced here: 88 us
  Pallas kernels  87.3 us (99%)
    pallas_call x1, Pallas kernels, body(): pl.pallas_call(functools.partial(system_kernel, n, nt), out_shape=(state,...  83.5 us
    pallas_call x1, Pallas kernels, body(): pl.pallas_call(finish_kernel, grid=(steps,), out_shape=(state, reports, s...  3.79 us

profile of v3, /device:TPU:1, one launch (start us, length us, event | category | flops | bytes accessed | tf_op | source)
XLA Modules:
  0.0 88.0 jit_solution(14501502612427713167)
XLA Ops:
  0.6 83.5 %shard_map.145 = (f32[2560,128]{1,0:T(8,128)S(1)}, f32[2560,128]{1,0:T(8,128)S(1)}, f32[2560,128]{1,0:T(8,128)S(1)}, f32[2560,128]{1,0:T(8,128)S(1)}, f32[2560,1...) custom-call(f32[2560,128]{1,0:T(8,128)} %bitcast.40, ...), custom_call_target="tpu_custom_call" | custom-call | flops 40000000000 | bytes 10000000 | tf_op jit(solution)/shard_map/pallas_call | solution.py:642
  84.1 3.8 %shard_map.146 = (f32[2560,128]{1,0:T(8,128)}, f32[512,128]{1,0:T(8,128)}, f32[2560,128]{1,0:T(8,128)}, f32[2560,128]{1,0:T(8,128)}, f32[512,128]{1,0:T(8,128)}, /*index=5*/f32[2560,128]{1,0:T(8,128)}) custom-call(f32[8,128]{1,0:T(8,128)S(1)} %get-tuple-element.21.sc, f32[2560,128]{1,0:T(8,128)S(1)} %get-tuple-element.22.f_in, ...), custom_call_target="tpu_custom_call" | custom-call | tf_op jit(solution)/shard_map/pallas_call | solution.py:674

commit v4 on v3

--- a/solution.py
+++ b/solution.py
@@ -15,6 +15,7 @@
 SLOTS = 2 * ROWS
 CELLS = LAT * WIDTH
 HALO, EDGE = 16, 8
+INNER = 8
 LAST = 8
 GROUPS = ((0, 4), (4, 4), (8, 2))
 
@@ -64,7 +65,7 @@
     f_t, df_t, rf, rd, c_t, v1, closing, arr, z, yacc, ysplit, rowsplit, keyrow, keycol,
     wa, wf, jf, jt, p_mat, pt_mat, send_a, recv_a, send_b, recv_b, obs_s, obs_r,
     acc, red, redbuf, zred, zbuf,
-    in_s, a2a_ss, a2a_rs, z_ss, z_rs, h_ss, h_rs, vh_ss, vh_rs, zz_ss, zz_rs,
+    in_s, a2a_ss, a2a_rs, z_ss, z_rs, h_ss, h_rs, vh_ss, vh_rs, zz_ss, zz_rs, r_ss, r_rs,
 ):
     cap = SLOTS // n
     s, c = lax.axis_index("tm"), lax.axis_index("col")
@@ -139,6 +140,10 @@
     def _(d):
         greet((lax.rem(s + d, nt), c))
 
+        @pl.loop(1, n // INNER)
+        def _(e):
+            greet((lax.rem(s + d, nt), lax.rem(c + e * INNER, n)))
+
     @pl.loop(1, n)
     def _(d):
         greet((s, lax.rem(c + d, n)))
@@ -154,6 +159,13 @@
     def _(y):
         for xt in range(2):
             f_t[8 + y, pl.ds(xt * 128, 128), :] = load_last(f_in, y, xt).T
+
+    pl.semaphore_wait(barrier, n + nt + (nt - 1) * (n // INNER - 1))
+    f_halo = z_halo(f_t, rf, 0)
+    f_halo.start()
+    f_send = z_send(f_t, rf, 0, (prev_s, c))
+    for i in (2, 0, 1):
+        f_send[i].start()
 
     rows_iota = lax.broadcasted_iota(I32, (ROWS, ROWS), 0)
     lane_iota = lax.broadcasted_iota(I32, (ROWS, ROWS), 1)
@@ -212,12 +224,6 @@
         b = o // lots
         send_a[o, 0:8, :] = keys[0:8, b * 128:(b + 1) * 128]
 
-    pl.semaphore_wait(barrier, n + nt)
-    f_halo = z_halo(f_t, rf, 0)
-    f_halo.start()
-    f_send = z_send(f_t, rf, 0, (prev_s, c))
-    for copy in f_send:
-        copy.start()
     exchange_start(0, send_a, recv_a)
 
     acc[...] = jnp.zeros_like(acc)
@@ -441,10 +447,12 @@
         each_pair(i, forward)
         closings[i].start()
 
+    first_adjoint(2)
     first_adjoint(0)
+    first_forward(2)
+    first_forward(0)
     exchange_wait(3, send_b, recv_b)
     z_edge2 = scatter(1, recv_b[...])
-    first_forward(0)
     first_adjoint(1)
 
     @pl.loop(0, 10)
@@ -459,8 +467,6 @@
     acc[1] += folded(wrd * wrd)
 
     first_forward(1)
-    first_adjoint(2)
-    first_forward(2)
 
     @pl.loop(0, STEPS * LAT)
     def _(i):
@@ -523,11 +529,11 @@
             acc[3] += folded(df * pu)
             acc[4] += folded(pu * pu)
 
+    arrive(2)
+    upper(2)
+    second_adjoint(0)
     arrive(0)
     upper(0)
-    second_adjoint(0)
-    arrive(1)
-    upper(1)
     second_adjoint(1)
     exchange_wait(1, obs_s, obs_r)
     right = jnp.concatenate(split2(obs_r[...].reshape(SLOTS, 128)), axis=1)
@@ -538,42 +544,43 @@
     acc[3] += folded(wrd * pm)
     acc[4] += folded(pm * pm)
 
-    arrive(2)
-    upper(2)
+    arrive(1)
+    upper(1)
     second_adjoint(2)
 
     lines = [jnp.sum(acc[i], axis=0, keepdims=True) for i in range(5)]
     red[...] = jnp.concatenate(lines + [jnp.zeros((3, 128), F32)], axis=0)
 
+    place_in, place_out = lax.rem(c, INNER), s * (n // INNER) + c // INNER
+    first = c - place_in
+
     def share(d):
+        to = lax.rem(place_in + d, INNER)
+        return rcopy(red, redbuf.at[place_in], r_ss.at[d], r_rs.at[d], (s, first + to))
+
+    for d in range(1, INNER):
+        share(d).start()
+    redbuf[place_in] = red[...]
+    for d in range(1, INNER):
+        peer = lax.rem(place_in + INNER - d, INNER)
+        rcopy(red, redbuf.at[peer], r_ss.at[d], r_rs.at[d], (s, first + peer)).wait_recv()
+    zred[...] = jnp.sum(redbuf[...], axis=0)
+    outer = n * nt // INNER
+
+    def share_out(d):
+        to = lax.rem(place_out + d, outer)
+        where = (to // (n // INNER), lax.rem(to, n // INNER) * INNER + place_in)
         return rcopy(
-            red, redbuf.at[c], a2a_ss.at[2, d], a2a_rs.at[2, d], (s, lax.rem(c + d, n))
-        )
-
-    @pl.loop(1, n)
-    def _(d):
-        share(d).start()
-
-    redbuf[c] = red[...]
-
-    @pl.loop(1, n)
-    def _(d):
-        peer = lax.rem(c + n - d, n)
-        rcopy(red, redbuf.at[peer], a2a_ss.at[2, d], a2a_rs.at[2, d], (s, peer)).wait_recv()
-
-    zred[...] = jnp.sum(redbuf[...], axis=0)
-
-    def share_z(d):
-        return rcopy(
-            zred, zbuf.at[s], z_ss.at[6 + d], z_rs.at[6 + d], (lax.rem(s + d, nt), c)
-        )
-
-    for d in range(1, nt):
-        share_z(d).start()
-    zbuf[s] = zred[...]
-    for d in range(1, nt):
-        peer = lax.rem(s + nt - d, nt)
-        rcopy(zred, zbuf.at[peer], z_ss.at[6 + d], z_rs.at[6 + d], (peer, c)).wait_recv()
+            zred, zbuf.at[place_out], r_ss.at[INNER + d], r_rs.at[INNER + d], where
+        )
+
+    for d in range(1, outer):
+        share_out(d).start()
+    zbuf[place_out] = zred[...]
+    for d in range(1, outer):
+        peer = lax.rem(place_out + outer - d, outer)
+        where = (peer // (n // INNER), lax.rem(peer, n // INNER) * INNER + place_in)
+        rcopy(zred, zbuf.at[peer], r_ss.at[INNER + d], r_rs.at[INNER + d], where).wait_recv()
 
     total = jnp.sum(jnp.sum(zbuf[...], axis=0), axis=1, keepdims=True)
     total = jnp.broadcast_to(total, (8, 128))
@@ -587,30 +594,50 @@
     for i, src, dst in ((0, send_a, recv_a), (1, obs_s, obs_r), (3, send_b, recv_b)):
         exchange_sent(i, src, dst)
 
-    @pl.loop(1, n)
-    def _(d):
+    for d in range(1, INNER):
         share(d).wait_send()
-
-    for d in range(1, nt):
-        share_z(d).wait_send()
+    for d in range(1, outer):
+        share_out(d).wait_send()
     for copy in [f_halo, d_halo, c_west, c_east, z_edge1, z_edge2] + f_send + d_send:
         copy.wait_send()
     for copy in edges + closings:
         copy.wait_send()
 
 
-def finish_kernel(sc, f_in, d_in, v1, v2, pu, wd_in, wrd_in, pm, ms, rs, xs, mr, rr, xr):
+def finish_kernel(
+    sc, f_in, d_in, v1, v2, pu, wd_in, wrd_in, pm,
+    ms_out, rs_out, xs_out, mr_out, rr_out, xr_out,
+    ms, rs, xs, mr, rr, xr, sem,
+):
     t, q = sc[0:1, :], sc[1:2, :]
-    f, d = f_in[...], d_in[...]
-    df = f * d
-    ms[...] = t * f - q * df
-    mr[...] = f - t * df + q * pu[...]
-    v = v1[...]
-    xs[...] = -(q * v)
-    xr[...] = q * v2[...] - t * v
+    parts = 5
+    size = ms.shape[0] // parts
+    copies = []
+
+    def send(i, src, dst):
+        copy = pltpu.make_async_copy(src, dst, sem.at[i])
+        copy.start()
+        copies.append(copy)
+
+    for i in range(parts):
+        rows = pl.ds(i * size, size)
+        f, v = f_in[rows, :], v1[rows, :]
+        df = f * d_in[rows, :]
+        ms[rows, :] = t * f - q * df
+        mr[rows, :] = f - t * df + q * pu[rows, :]
+        xs[rows, :] = -(q * v)
+        xr[rows, :] = q * v2[rows, :] - t * v
+        for j, (src, dst) in enumerate(
+            ((ms, ms_out), (mr, mr_out), (xs, xs_out), (xr, xr_out))
+        ):
+            send(4 * i + j, src.at[rows, :], dst.at[rows, :])
     wd, wrd = wd_in[...], wrd_in[...]
     rs[...] = t * wd - q * wrd
     rr[...] = wd - t * wrd + q * pm[...]
+    send(4 * parts, rs, rs_out)
+    send(4 * parts + 1, rr, rr_out)
+    for copy in copies:
+        copy.wait()
 
 
 def to_rows(x):
@@ -657,10 +684,11 @@
             V((n, 8 + cap, 128), F32), V((n, 8 + cap, 128), F32),
             V((n, cap, 128), F32), V((n, cap, 128), F32),
             V((n, cap, 128), F32), V((n, cap, 128), F32),
-            V((5, 8, 128), F32), V((8, 128), F32), V((n, 8, 128), F32),
-            V((8, 128), F32), V((nt, 8, 128), F32),
-            dma((10,)), dma((4, n)), dma((4, n)), dma((6 + nt,)), dma((6 + nt,)),
+            V((5, 8, 128), F32), V((8, 128), F32), V((INNER, 8, 128), F32),
+            V((8, 128), F32), V((n * nt // INNER, 8, 128), F32),
+            dma((10,)), dma((4, n)), dma((4, n)), dma((6,)), dma((6,)),
             dma((6,)), dma((6,)), dma((3,)), dma((3,)), dma((3,)), dma((3,)),
+            dma((INNER + n * nt // INNER,)), dma((INNER + n * nt // INNER,)),
         ],
         compiler_params=pltpu.CompilerParams(
             collective_id=0, has_side_effects=True, vmem_limit_bytes=42 * 1024 * 1024
@@ -668,16 +696,14 @@
         cost_estimate=pl.CostEstimate(flops=40 * 10**9, bytes_accessed=10**7, transcendentals=0),
     )(*inputs)
     fv, dv, v1, v2, pu, wd, wrd, pm, sc = results
-    steps = 8
-    part = pl.BlockSpec((size // steps, 128), lambda i: (i, 0))
-    rpart = pl.BlockSpec((ROWS // steps, CHANNELS), lambda i: (i, 0))
+    outs = (state, reports, state, state, reports, state)
     ms, rs, xs, mr, rr, xr = pl.pallas_call(
         finish_kernel,
-        grid=(steps,),
-        out_shape=(state, reports, state, state, reports, state),
-        in_specs=[pl.BlockSpec((8, 128), lambda i: (0, 0))] + [part] * 5 + [rpart] * 3,
-        out_specs=(part, rpart, part, part, rpart, part),
-        compiler_params=pltpu.CompilerParams(vmem_limit_bytes=32 * 1024 * 1024),
+        out_shape=outs,
+        in_specs=[vmem] * 9,
+        out_specs=(pl.BlockSpec(memory_space=pl.ANY),) * 6,
+        scratch_shapes=[V(x.shape, x.dtype) for x in outs] + [dma((22,))],
+        compiler_params=pltpu.CompilerParams(vmem_limit_bytes=16 * 1024 * 1024),
     )(sc, fv, dv, v1, v2, pu, wd, wrd, pm)
     shape = forcing_state.shape[1:]
     ms, xs, mr, xr = (from_rows(x, shape)[None] for x in (ms, xs, mr, xr))

time: 88.1 us -> 84.9 us (0.964)
  Pallas kernels: 87.3 us -> 84 us
    pallas_call x1, Pallas kernels: 83.5 us -> 81.3 us  [body(): pl.pallas_call(functools.partial(system_kernel, n, nt), out_shape=(state,...]
    pallas_call x1, Pallas kernels: 3.79 us -> 2.72 us  [body(): pl.pallas_call(finish_kernel, out_shape=outs, in_specs=[vmem] * 9, out_sp...]
where the time goes in v4:
time: 84.9 us; the launch traced here: 84.8 us
  Pallas kernels  84 us (99%)
    pallas_call x1, Pallas kernels, body(): pl.pallas_call(functools.partial(system_kernel, n, nt), out_shape=(state,...  81.3 us
    pallas_call x1, Pallas kernels, body(): pl.pallas_call(finish_kernel, out_shape=outs, in_specs=[vmem] * 9, out_sp...  2.72 us

profile of v4, /device:TPU:1, one launch (start us, length us, event | category | flops | bytes accessed | tf_op | source)
XLA Modules:
  0.0 84.8 jit_solution(14891358569254082637)
XLA Ops:
  0.6 81.3 %shard_map.145 = (f32[2560,128]{1,0:T(8,128)S(1)}, f32[2560,128]{1,0:T(8,128)S(1)}, f32[2560,128]{1,0:T(8,128)S(1)}, f32[2560,128]{1,0:T(8,128)S(1)}, f32[2560,1...) custom-call(f32[2560,128]{1,0:T(8,128)} %bitcast.40, ...), custom_call_target="tpu_custom_call" | custom-call | flops 40000000000 | bytes 10000000 | tf_op jit(solution)/shard_map/pallas_call | solution.py:669
  82.0 2.7 %shard_map.146 = (f32[2560,128]{1,0:T(8,128)}, f32[512,128]{1,0:T(8,128)}, f32[2560,128]{1,0:T(8,128)}, f32[2560,128]{1,0:T(8,128)}, f32[512,128]{1,0:T(8,128)}, /*index=5*/f32[2560,128]{1,0:T(8,128)}) custom-call(f32[8,128]{1,0:T(8,128)S(1)} %get-tuple-element.21.sc, f32[2560,128]{1,0:T(8,128)S(1)} %get-tuple-element.22.f_in, ...), custom_call_target="tpu_custom_call" | custom-call | tf_op jit(solution)/shard_map/pallas_call | solution.py:700

commit v5 on v4

--- a/solution.py
+++ b/solution.py
@@ -94,31 +94,21 @@
             h_ss.at[i], h_rs.at[i], (prev_s, west),
         )
 
-    def exchange(i, src, dst, d):
-        peer = lax.rem(c + d, n)
-        return rcopy(
-            src.at[peer], dst.at[c], a2a_ss.at[i, d], a2a_rs.at[i, d], (s, peer)
-        )
-
     def exchange_start(i, src, dst):
-        @pl.loop(1, n)
-        def _(d):
-            exchange(i, src, dst, d).start()
-
+        for d in range(1, n):
+            peer = (c + d) & (n - 1)
+            rcopy(src.at[peer], dst.at[c], a2a_ss.at[i], a2a_rs.at[i], (s, peer)).start()
         dst[c] = src[c]
 
+    def exchange_all(i, src, dst):
+        every = pl.ds(0, n - 1)
+        return rcopy(src.at[every], dst.at[every], a2a_ss.at[i], a2a_rs.at[i], (s, east))
+
     def exchange_wait(i, src, dst):
-        @pl.loop(1, n)
-        def _(d):
-            peer = lax.rem(c + n - d, n)
-            rcopy(
-                src.at[peer], dst.at[peer], a2a_ss.at[i, d], a2a_rs.at[i, d], (s, peer)
-            ).wait_recv()
+        exchange_all(i, src, dst).wait_recv()
 
     def exchange_sent(i, src, dst):
-        @pl.loop(1, n)
-        def _(d):
-            exchange(i, src, dst, d).wait_send()
+        exchange_all(i, src, dst).wait_send()
 
     pairs = (
         (f_hbm, f_in), (col_hbm, col), (slot_hbm, slot), (cnt_hbm, cnt), (inn_hbm, inn),
@@ -257,7 +247,7 @@
     )
     c_west.start()
     c_east.start()
-    exchange_start(3, send_b, recv_b)
+    exchange_start(2, send_b, recv_b)
     loads[9].wait()
 
     @pl.loop(0, 8)
@@ -451,7 +441,7 @@
     first_adjoint(0)
     first_forward(2)
     first_forward(0)
-    exchange_wait(3, send_b, recv_b)
+    exchange_wait(2, send_b, recv_b)
     z_edge2 = scatter(1, recv_b[...])
     first_adjoint(1)
 
@@ -546,6 +536,12 @@
 
     arrive(1)
     upper(1)
+    for i, src, dst in ((0, send_a, recv_a), (1, obs_s, obs_r), (2, send_b, recv_b)):
+        exchange_sent(i, src, dst)
+    for copy in [f_halo, d_halo, c_west, c_east, z_edge1, z_edge2] + f_send:
+        copy.wait_send()
+    for copy in edges + closings:
+        copy.wait_send()
     second_adjoint(2)
 
     lines = [jnp.sum(acc[i], axis=0, keepdims=True) for i in range(5)]
@@ -591,16 +587,11 @@
         [step1 + step2, step1 * step2, jnp.zeros((6, 128), F32)], axis=0
     )
 
-    for i, src, dst in ((0, send_a, recv_a), (1, obs_s, obs_r), (3, send_b, recv_b)):
-        exchange_sent(i, src, dst)
-
     for d in range(1, INNER):
         share(d).wait_send()
     for d in range(1, outer):
         share_out(d).wait_send()
-    for copy in [f_halo, d_halo, c_west, c_east, z_edge1, z_edge2] + f_send + d_send:
-        copy.wait_send()
-    for copy in edges + closings:
+    for copy in d_send:
         copy.wait_send()
 
 
@@ -686,7 +677,7 @@
             V((n, cap, 128), F32), V((n, cap, 128), F32),
             V((5, 8, 128), F32), V((8, 128), F32), V((INNER, 8, 128), F32),
             V((8, 128), F32), V((n * nt // INNER, 8, 128), F32),
-            dma((10,)), dma((4, n)), dma((4, n)), dma((6,)), dma((6,)),
+            dma((10,)), dma((3,)), dma((3,)), dma((6,)), dma((6,)),
             dma((6,)), dma((6,)), dma((3,)), dma((3,)), dma((3,)), dma((3,)),
             dma((INNER + n * nt // INNER,)), dma((INNER + n * nt // INNER,)),
         ],

time: 84.9 us -> 82 us (0.966)
  Pallas kernels: 84 us -> 81.1 us
    pallas_call x1, Pallas kernels: 81.3 us -> 78.4 us  [body(): pl.pallas_call(functools.partial(system_kernel, n, nt), out_shape=(state,...]
where the time goes in v5:
time: 82 us; the launch traced here: 81.9 us
  Pallas kernels  81.1 us (99%)
    pallas_call x1, Pallas kernels, body(): pl.pallas_call(functools.partial(system_kernel, n, nt), out_shape=(state,...  78.4 us
    pallas_call x1, Pallas kernels, body(): pl.pallas_call(finish_kernel, out_shape=outs, in_specs=[vmem] * 9, out_sp...  2.72 us

profile of v5, /device:TPU:1, one launch (start us, length us, event | category | flops | bytes accessed | tf_op | source)
XLA Modules:
  0.0 81.9 jit_solution(14751954769645871101)
XLA Ops:
  0.6 78.4 %shard_map.145 = (f32[2560,128]{1,0:T(8,128)S(1)}, f32[2560,128]{1,0:T(8,128)S(1)}, f32[2560,128]{1,0:T(8,128)S(1)}, f32[2560,128]{1,0:T(8,128)S(1)}, f32[2560,1...) custom-call(f32[2560,128]{1,0:T(8,128)} %bitcast.40, ...), custom_call_target="tpu_custom_call" | custom-call | flops 40000000000 | bytes 10000000 | tf_op jit(solution)/shard_map/pallas_call | solution.py:660
  79.0 2.7 %shard_map.146 = (f32[2560,128]{1,0:T(8,128)}, f32[512,128]{1,0:T(8,128)}, f32[2560,128]{1,0:T(8,128)}, f32[2560,128]{1,0:T(8,128)}, f32[512,128]{1,0:T(8,128)}, /*index=5*/f32[2560,128]{1,0:T(8,128)}) custom-call(f32[8,128]{1,0:T(8,128)S(1)} %get-tuple-element.21.sc, f32[2560,128]{1,0:T(8,128)S(1)} %get-tuple-element.22.f_in, ...), custom_call_target="tpu_custom_call" | custom-call | tf_op jit(solution)/shard_map/pallas_call | solution.py:691

commit v6 on v5

--- a/solution.py
+++ b/solution.py
@@ -62,7 +62,7 @@
     f_hbm, d_hbm, c_hbm, vm_hbm, jac_hbm, inn_hbm, rvar_hbm, col_hbm, slot_hbm, cnt_hbm,
     f_in, d_in, v1n, v2n, pun, wd_out, wrd_out, pm_out, sc_out,
     c_in, vm, jac, inn, rvar, col, slot, cnt,
-    f_t, df_t, rf, rd, c_t, v1, closing, arr, z, yacc, ysplit, rowsplit, keyrow, keycol,
+    f_t, df_t, f_raw, rf, rd, c_t, v1, closing, arr, z, yacc, ysplit, rowsplit, keyrow, keycol,
     wa, wf, jf, jt, p_mat, pt_mat, send_a, recv_a, send_b, recv_b, obs_s, obs_r,
     acc, red, redbuf, zred, zbuf,
     in_s, a2a_ss, a2a_rs, z_ss, z_rs, h_ss, h_rs, vh_ss, vh_rs, zz_ss, zz_rs, r_ss, r_rs,
@@ -138,6 +138,16 @@
     def _(d):
         greet((s, lax.rem(c + d, n)))
 
+    pl.semaphore_wait(barrier, n + nt + (nt - 1) * (n // INNER - 1))
+
+    f_send = []
+    for i, (k0, kn) in enumerate(GROUPS):
+        rows = pl.ds(k0 * WIDTH, kn * WIDTH)
+        f_send.append(
+            rcopy(f_hbm.at[rows], f_raw.at[rows], z_ss.at[i], z_rs.at[i], (prev_s, c))
+        )
+    for i in (2, 0, 1):
+        f_send[i].start()
     loads[0].wait()
 
     @pl.loop(0, 8)
@@ -150,12 +160,8 @@
         for xt in range(2):
             f_t[8 + y, pl.ds(xt * 128, 128), :] = load_last(f_in, y, xt).T
 
-    pl.semaphore_wait(barrier, n + nt + (nt - 1) * (n // INNER - 1))
     f_halo = z_halo(f_t, rf, 0)
     f_halo.start()
-    f_send = z_send(f_t, rf, 0, (prev_s, c))
-    for i in (2, 0, 1):
-        f_send[i].start()
 
     rows_iota = lax.broadcasted_iota(I32, (ROWS, ROWS), 0)
     lane_iota = lax.broadcasted_iota(I32, (ROWS, ROWS), 1)
@@ -424,6 +430,13 @@
         f_send[i].wait_recv()
 
         def run(k, g, y):
+            for j in range(2):
+                for xt in range(2):
+                    half = pl.ds(xt * 128, 128)
+                    if g == 2:
+                        rf[k + j, half, :] = load_last(f_raw, y + j, xt).T
+                    else:
+                        rf[k + j, half, :] = load_pair(f_raw, g, y + j, xt).T
             for j, value in enumerate(adjoint(0, k, g, y, rf, f_t)):
                 v1[k + j, pl.ds(HALO, WIDTH), :] = value
                 acc[1] += folded(value * value)
@@ -490,7 +503,10 @@
                 own = v1[k + j, pl.ds(HALO, WIDTH), :]
                 acc[3] += folded(own * value)
                 acc[4] += folded(value * value)
-                put(v2n, k + j, g, y + j, value)
+                if g == 2:
+                    closing[k + j] = value
+                else:
+                    put(v2n, k + j, g, y + j, value)
 
         each_pair(i, run)
 
@@ -557,6 +573,8 @@
     for d in range(1, INNER):
         share(d).start()
     redbuf[place_in] = red[...]
+    for y in range(2):
+        put_last(v2n, y, closing[LAST + y])
     for d in range(1, INNER):
         peer = lax.rem(place_in + INNER - d, INNER)
         rcopy(red, redbuf.at[peer], r_ss.at[d], r_rs.at[d], (s, first + peer)).wait_recv()
@@ -663,7 +681,7 @@
         in_specs=[hbm] * 10,
         out_specs=(vmem,) * 9,
         scratch_shapes=[V(x.shape, x.dtype) for x in inputs[2:]] + [
-            V((10, WIDTH, 128), F32), V((10, WIDTH, 128), F32),
+            V((10, WIDTH, 128), F32), V((10, WIDTH, 128), F32), V((size, 128), F32),
             V((10, span, 128), F32), V((10, span, 128), F32),
             V((6 * STEPS, span + HALO, 128), F32),
             V((10, span, 128), F32), V((10, WIDTH, 128), F32), V((10, WIDTH, 128), F32),

time: 82 us -> 87.8 us (1.071)
  Pallas kernels: 81.1 us -> 86.9 us
    pallas_call x1, Pallas kernels: 78.4 us -> 84.2 us  [body(): pl.pallas_call(functools.partial(system_kernel, n, nt), out_shape=(state,...]
where the time goes in v6:
time: 87.8 us; the launch traced here: 87.7 us
  Pallas kernels  86.9 us (99%)
    pallas_call x1, Pallas kernels, body(): pl.pallas_call(functools.partial(system_kernel, n, nt), out_shape=(state,...  84.2 us
    pallas_call x1, Pallas kernels, body(): pl.pallas_call(finish_kernel, out_shape=outs, in_specs=[vmem] * 9, out_sp...  2.72 us

profile of v6, /device:TPU:1, one launch (start us, length us, event | category | flops | bytes accessed | tf_op | source)
XLA Modules:
  0.0 87.7 jit_solution(11567621835767654611)
XLA Ops:
  0.6 84.2 %shard_map.145 = (f32[2560,128]{1,0:T(8,128)S(1)}, f32[2560,128]{1,0:T(8,128)S(1)}, f32[2560,128]{1,0:T(8,128)S(1)}, f32[2560,128]{1,0:T(8,128)S(1)}, f32[2560,1...) custom-call(f32[2560,128]{1,0:T(8,128)} %bitcast.40, ...), custom_call_target="tpu_custom_call" | custom-call | flops 40000000000 | bytes 10000000 | tf_op jit(solution)/shard_map/pallas_call | solution.py:678
  84.8 2.7 %shard_map.146 = (f32[2560,128]{1,0:T(8,128)}, f32[512,128]{1,0:T(8,128)}, f32[2560,128]{1,0:T(8,128)}, f32[2560,128]{1,0:T(8,128)}, f32[512,128]{1,0:T(8,128)}, /*index=5*/f32[2560,128]{1,0:T(8,128)}) custom-call(f32[8,128]{1,0:T(8,128)S(1)} %get-tuple-element.21.sc, f32[2560,128]{1,0:T(8,128)S(1)} %get-tuple-element.22.f_in, ...), custom_call_target="tpu_custom_call" | custom-call | tf_op jit(solution)/shard_map/pallas_call | solution.py:709

commit v7 on v5

--- a/solution.py
+++ b/solution.py
@@ -149,13 +149,6 @@
     def _(y):
         for xt in range(2):
             f_t[8 + y, pl.ds(xt * 128, 128), :] = load_last(f_in, y, xt).T
-
-    pl.semaphore_wait(barrier, n + nt + (nt - 1) * (n // INNER - 1))
-    f_halo = z_halo(f_t, rf, 0)
-    f_halo.start()
-    f_send = z_send(f_t, rf, 0, (prev_s, c))
-    for i in (2, 0, 1):
-        f_send[i].start()
 
     rows_iota = lax.broadcasted_iota(I32, (ROWS, ROWS), 0)
     lane_iota = lax.broadcasted_iota(I32, (ROWS, ROWS), 1)
@@ -214,6 +207,12 @@
         b = o // lots
         send_a[o, 0:8, :] = keys[0:8, b * 128:(b + 1) * 128]
 
+    pl.semaphore_wait(barrier, n + nt + (nt - 1) * (n // INNER - 1))
+    f_halo = z_halo(f_t, rf, 0)
+    f_halo.start()
+    f_send = z_send(f_t, rf, 0, (prev_s, c))
+    for i in (2, 0, 1):
+        f_send[i].start()
     exchange_start(0, send_a, recv_a)
 
     acc[...] = jnp.zeros_like(acc)
@@ -490,7 +489,10 @@
                 own = v1[k + j, pl.ds(HALO, WIDTH), :]
                 acc[3] += folded(own * value)
                 acc[4] += folded(value * value)
-                put(v2n, k + j, g, y + j, value)
+                if g == 2:
+                    closing[k + j] = value
+                else:
+                    put(v2n, k + j, g, y + j, value)
 
         each_pair(i, run)
 
@@ -557,6 +559,8 @@
     for d in range(1, INNER):
         share(d).start()
     redbuf[place_in] = red[...]
+    for y in range(2):
+        put_last(v2n, y, closing[LAST + y])
     for d in range(1, INNER):
         peer = lax.rem(place_in + INNER - d, INNER)
         rcopy(red, redbuf.at[peer], r_ss.at[d], r_rs.at[d], (s, first + peer)).wait_recv()

time: 82 us -> 83.9 us (1.023)
  Pallas kernels: 81.1 us -> 83 us
    pallas_call x1, Pallas kernels: 78.4 us -> 80.3 us  [body(): pl.pallas_call(functools.partial(system_kernel, n, nt), out_shape=(state,...]
where the time goes in v7:
time: 83.9 us; the launch traced here: 83.8 us
  Pallas kernels  83 us (99%)
    pallas_call x1, Pallas kernels, body(): pl.pallas_call(functools.partial(system_kernel, n, nt), out_shape=(state,...  80.3 us
    pallas_call x1, Pallas kernels, body(): pl.pallas_call(finish_kernel, out_shape=outs, in_specs=[vmem] * 9, out_sp...  2.72 us

profile of v7, /device:TPU:1, one launch (start us, length us, event | category | flops | bytes accessed | tf_op | source)
XLA Modules:
  0.0 83.8 jit_solution(17847172962041527002)
XLA Ops:
  0.6 80.3 %shard_map.145 = (f32[2560,128]{1,0:T(8,128)S(1)}, f32[2560,128]{1,0:T(8,128)S(1)}, f32[2560,128]{1,0:T(8,128)S(1)}, f32[2560,128]{1,0:T(8,128)S(1)}, f32[2560,1...) custom-call(f32[2560,128]{1,0:T(8,128)} %bitcast.40, ...), custom_call_target="tpu_custom_call" | custom-call | flops 40000000000 | bytes 10000000 | tf_op jit(solution)/shard_map/pallas_call | solution.py:664
  80.9 2.7 %shard_map.146 = (f32[2560,128]{1,0:T(8,128)}, f32[512,128]{1,0:T(8,128)}, f32[2560,128]{1,0:T(8,128)}, f32[2560,128]{1,0:T(8,128)}, f32[512,128]{1,0:T(8,128)}, /*index=5*/f32[2560,128]{1,0:T(8,128)}) custom-call(f32[8,128]{1,0:T(8,128)S(1)} %get-tuple-element.21.sc, f32[2560,128]{1,0:T(8,128)S(1)} %get-tuple-element.22.f_in, ...), custom_call_target="tpu_custom_call" | custom-call | tf_op jit(solution)/shard_map/pallas_call | solution.py:695
